TPU v7x, 128 devices: a whole 4x4x4 slice. The times are simulated.
128 devices in a mesh: side: 2 (over core), row: 8 (over z_hi, y), col: 8 (over z_lo, x).
Axes of the slice: x: 4, y: 4, z: 4 (z_hi: 2, z_lo: 2; z = z_hi * 2 + z_lo), core: 2. Of those that a mesh axis runs over, the one named last changes fastest.
Arguments:
- queries: bfloat16 [1024, 128, 576], P(('side', 'row'), 'col'), may hold values from -48 to 48
- cache: bfloat16 [1024, 128, 576], P(('side', 'row')), may hold values from -4 to 4
- lengths: int32 [1024], P(('side', 'row')), may hold values from 2 to 128, as said below
- w_uv: bfloat16 [128, 512, 128], P('col'), may hold values from -0.25 to 0.25
- w_out: bfloat16 [16384, 7168], P('col', ('side', 'row')), may hold values from -0.046875 to 0.046875
- residual_in: bfloat16 [1024, 7168], P('col', ('side', 'row')), may hold values from -8 to 8
- norm_gain: bfloat16 [7168], P(('side', 'row')), may hold values from 0.099609375 to 1.8984375
- expert_ids: int32 [1024, 8], P('col'), may hold values from 0 to 15, all different within a row; in each aligned block of 128 rows (0 to 127, 128 to 255, ...) at most 96 rows name the same one
- gate_vals: float32 [1024, 8], P('col'), may hold values from 0.05 to 0.5
- w_gate: bfloat16 [16, 7168, 2048], P(('side', 'row'), None, 'col'), may hold values from -0.0625 to 0.0625
- w_up: bfloat16 [16, 7168, 2048], P(('side', 'row'), None, 'col'), may hold values from -0.0625 to 0.0625
- w_down: bfloat16 [16, 2048, 7168], P(('side', 'row'), 'col'), may hold values from -0.125 to 0.125
Outputs:
- mixed: bfloat16 [1024, 7168], P('col', ('side', 'row'))
Inputs may be any that keep to these rules, and one draw needn't show every extreme that they name: Row b's cache holds its keys in slots below lengths[b]; some row has all 128 slots live. `expert_ids`: each row names 8 different experts; within each aligned block of 128 rows no expert is named by more than 96 rows.
All inputs are finite; a program needn't handle non-finite values.
Results may differ from a plain program's by a relative error of at most 0.015.
Values may be sent and summed in bfloat16 or wider, within the bound.
A program may use at most 192 MiB of HBM per device.

v0:
```python
import jax
import jax.numpy as jnp
from jax import lax
from jax.sharding import PartitionSpec as P

D = 7168
ROPE = 64
HD = 128


def shards(
    queries,
    cache,
    lengths,
    w_uv,
    w_out,
    residual_in,
    norm_gain,
    expert_ids,
    gate_vals,
    w_gate,
    w_up,
    w_down,
):
    score_scale = (HD + ROPE) ** (-0.5)
    scores = (
        jnp.einsum("rhk,rlk->rhl", queries, cache, preferred_element_type=jnp.float32) * score_scale
    )
    places = lax.broadcasted_iota(jnp.int32, (1, 1, cache.shape[1]), 2)
    scores = jnp.where(places < lengths[:, None, None], scores, -jnp.inf)
    row_top = jnp.max(scores, axis=2, keepdims=True)
    exp_terms = jnp.exp(scores - row_top)
    attn_probs = (exp_terms / jnp.sum(exp_terms, axis=2, keepdims=True)).astype(jnp.bfloat16)
    latent_width = w_uv.shape[1]
    latent = jnp.einsum(
        "rhl,rlk->rhk", attn_probs, cache[:, :, :latent_width], preferred_element_type=jnp.float32
    ).astype(jnp.bfloat16)
    head_out = jnp.einsum("rhk,hkd->rhd", latent, w_uv, preferred_element_type=jnp.float32).astype(
        jnp.bfloat16
    )
    head_out = head_out.reshape(head_out.shape[0], -1)
    partial_rows = jnp.dot(
        lax.all_gather(head_out, ("side", "row"), axis=0, tiled=True),
        w_out,
        preferred_element_type=jnp.float32,
    )
    attn_slice = lax.psum_scatter(
        partial_rows.astype(jnp.bfloat16), "col", scatter_dimension=0, tiled=True
    ).astype(jnp.float32)
    hidden = residual_in.astype(jnp.float32) + attn_slice
    squares_total = lax.psum(jnp.sum(hidden * hidden, axis=1), ("side", "row"))
    inverse = lax.rsqrt(squares_total / D + 1e-06)
    normed = (hidden * inverse[:, None] * norm_gain.astype(jnp.float32)).astype(jnp.bfloat16)
    owner_index = lax.axis_index(("side", "row"))
    chosen = expert_ids == owner_index
    my_gate = jnp.sum(jnp.where(chosen, gate_vals, 0.0), axis=1)
    gate_dev = w_gate[0]
    up_dev = w_up[0]
    down_dev = w_down[0]
    full_block = lax.all_gather(normed, ("side", "row"), axis=1, tiled=True)
    row_piece = lax.all_gather(full_block, "col", axis=0, tiled=True)
    gate_part = jnp.dot(row_piece, gate_dev, preferred_element_type=jnp.float32)
    up_part = jnp.dot(row_piece, up_dev, preferred_element_type=jnp.float32)
    activations = (jax.nn.silu(gate_part) * up_part).astype(jnp.bfloat16)
    expert_rows = lax.psum_scatter(
        jnp.dot(activations, down_dev, preferred_element_type=jnp.float32).astype(jnp.bfloat16),
        "col",
        scatter_dimension=0,
        tiled=True,
    ).astype(jnp.float32)
    weighted = my_gate[:, None] * expert_rows
    expert_total = lax.psum_scatter(
        weighted.astype(jnp.bfloat16), ("side", "row"), scatter_dimension=1, tiled=True
    ).astype(jnp.float32)
    return (hidden + expert_total).astype(jnp.bfloat16)


def solution(mesh):
    placed = (
        P(("side", "row"), "col", None),
        P(("side", "row"), None, None),
        P(("side", "row")),
        P("col", None, None),
        P("col", ("side", "row")),
        P("col", ("side", "row")),
        P(("side", "row")),
        P("col", None),
        P("col", None),
        P(("side", "row"), None, "col"),
        P(("side", "row"), None, "col"),
        P(("side", "row"), "col", None),
    )
    return jax.shard_map(
        shards, mesh=mesh, in_specs=placed, out_specs=P("col", ("side", "row")), check_vma=False
    )
```

profile of v0, /device:TPU:1, one launch (start us, length us, event | category | flops | bytes accessed | tf_op | source)
XLA Modules:
  0.0 629.2 jit_solution(10705832504107198747)
XLA Ops:
  6.5 0.0 copy-start
  6.5 0.0 all-gather.4.cloned.1.call-start
  6.5 0.9 iota_compare_fusion
  7.4 5.6 fusion.18
  13.0 0.3 fusion.24
  13.4 6.7 %fusion.8 = bf16[64,16,512]{2,1,0:T(8,128)(2,1)} fusion(bf16[64,128,576]{1,2,0:T(8,128)(2,1)} %param.13, f32[64,16]{1,0:T(8,128)S(1)} %fusion.24, f32[64,16,128]{2,1,0:T(8,128)S(1)} %fusion.18), kind=kOutput, calls=%fused_computation.10 | convolution fusion | flops 135136384 | bytes 10518528 | tf_op jit(solution)/shard_map/rhl,rlk->rhk/dot_general | solution.py:35
  20.1 0.0 copy-done
  20.1 2.5 fusion.20
  22.6 0.7 copy.29
  23.4 0.0 all-gather.4.cloned.1.call-update
  23.4 0.0 copy-start.7
  23.4 0.0 copy-start.4
  23.4 0.0 reduce-scatter.10.cloned.1.call-start
  23.5 59.8 %all-gather.4.cloned.1.call-done = bf16[1024,2048]{1,0:T(8,128)(2,1)} async-done(((bf16[64,2048]{1,0:T(8,128)(2,1)}), bf16[1024,2048]{1,0:T(8,128)(2,1)}) %all-gather.4.cloned.1.call-update) | async-done | bytes 4194320 | tf_op jit(solution)/shard_map/all_gather | solution.py:43
  83.3 4.9 convolution_convert_fusion.1
  88.2 1.3 copy.20
  89.5 0.0 reduce-scatter.10.cloned.1.call-update
  89.5 0.0 all-gather.6.cloned.1.call-start
  89.6 0.0 copy-done.7
  89.6 32.5 %reduce-scatter.10.cloned.1.call-done = bf16[128,448]{1,0:T(8,128)(2,1)} async-done(((bf16[1024,448]{1,0:T(8,128)(2,1)}), bf16[128,448]{1,0:T(8,128)(2,1)}) %reduce-scatter.10.cloned.1.call-update) | async-done | bytes 114704
  122.1 1.0 copy.21
  123.1 0.0 copy-done.4
  123.2 0.1 multiply_reduce_fusion
  123.2 43.3 %psum.7 = f32[128]{0:T(128)S(1)} all-reduce(f32[128]{0:T(128)S(1)} %multiply_reduce_fusion), channel_id=1, replica_groups=mesh['side'=2,'row'=8,'col'=8] {'side','row'}, use_global_device_ids=true, to_apply=%region_5.6 | all-reduce | flops 128 | bytes 1024 | tf_op jit(solution)/shard_map/psum | solution.py:51
  166.5 0.8 multiply_convert_fusion.1
  167.3 0.0 all-gather.6.cloned.1.call-update
  167.3 0.0 all-gather.8.cloned.1.call-start
  167.4 46.0 %all-gather.6.cloned.1.call-done = bf16[128,7168]{0,1:T(8,128)(2,1)} async-done(((bf16[128,448]{0,1:T(8,128)(2,1)}), bf16[128,7168]{0,1:T(8,128)(2,1)}) %all-gather.6.cloned.1.call-update) | async-done | bytes 1835024 | tf_op jit(solution)/shard_map/all_gather | solution.py:60
  213.4 0.0 all-gather.8.cloned.1.call-update
  213.4 0.2 reduce-scatter.12.cloned.1.call-start
  213.6 153.7 %all-gather.8.cloned.1.call-done = bf16[1024,7168]{0,1:T(8,128)(2,1)} async-done(((bf16[128,7168]{0,1:T(8,128)(2,1)}), bf16[1024,7168]{0,1:T(8,128)(2,1)}) %all-gather.8.cloned.1.call-update) | async-done | bytes 14680080 | tf_op jit(solution)/shard_map/all_gather | solution.py:61
  367.3 8.5 %fusion.6 = f32[1024,256]{1,0:T(8,128)S(1)} fusion(bf16[1024,7168]{0,1:T(8,128)(2,1)} %all-gather.8.cloned.1.call-done, bf16[1,7168,256]{2,1,0:T(8,128)(2,1)} %param.21), kind=kOutput, calls=%fused_computation.7 | convolution fusion | flops 3758096384 | bytes 19398656 | tf_op jit(solution)/shard_map/dot_general | solution.py:62
  375.8 1.9 copy-done.2
  377.7 1.0 copy-done.8
  378.7 4.1 fusion.14
  382.8 0.0 copy-done.3
  382.8 7.3 %convolution_convert_fusion = bf16[1024,7168]{1,0:T(8,128)(2,1)} fusion(bf16[1024,256]{1,0:T(8,128)(2,1)S(1)} %fusion.14, bf16[1,256,7168]{2,1,0:T(8,128)(2,1)S(1)} %copy-done.3), kind=kOutput, calls=%fused_computation.1 | convolution fusion | flops 3765436416 | bytes 18874368 | tf_op jit(solution)/shard_map/dot_general | solution.py:66
  390.1 0.0 reduce-scatter.12.cloned.1.call-update
  390.1 0.0 reduce-scatter.8.cloned.1.call-start
  390.2 0.6 copy-done.5
  390.8 0.0 copy-done.6
  390.8 155.8 %reduce-scatter.12.cloned.1.call-done = bf16[128,7168]{1,0:T(8,128)(2,1)} async-done(((bf16[1024,7168]{1,0:T(8,128)(2,1)}), bf16[128,7168]{1,0:T(8,128)(2,1)}) %reduce-scatter.12.cloned.1.call-update) | async-done | bytes 1835024
  546.7 4.1 copy.23
  550.7 3.1 multiply_convert_fusion
  553.8 0.0 reduce-scatter.8.cloned.1.call-update
  553.9 66.9 %reduce-scatter.8.cloned.1.call-done = bf16[128,448]{0,1:T(8,128)(2,1)} async-done(((bf16[128,7168]{0,1:T(8,128)(2,1)}), bf16[128,448]{0,1:T(8,128)(2,1)}) %reduce-scatter.8.cloned.1.call-update) | async-done | bytes 114704 | tf_op jit(solution)/shard_map/reduce_scatter | solution.py:72
  620.8 1.6 add_convert_fusion
  622.4 0.0 copy-done.1
  (9 shorter events, 0.0 us)
Async XLA Ops:
  6.5 13.6 %copy-start = (bf16[16,512,128]{2,1,0:T(8,128)(2,1)S(1)}, bf16[16,512,128]{2,1,0:T(8,128)(2,1)}, u32[]{:S(2)}) copy-start(bf16[16,512,128]{2,1,0:T(8,128)(2,1)} %param.15) | copy-start | bytes 6291460
  6.5 76.8 %all-gather.4.cloned.1.call-start = ((), (), s32[]{:S(2)}) async-start(), calls=%async_computation.3 | async-start | bytes 4456448 | tf_op jit(solution)/shard_map/all_gather | solution.py:43
  23.4 66.2 %copy-start.7 = (bf16[448]{0:T(512)(128)(2,1)S(1)}, bf16[448]{0:T(512)(128)(2,1)}, u32[]{:S(2)}) copy-start(bf16[448]{0:T(512)(128)(2,1)} %param.18) | copy-start | bytes 2692
  23.4 99.7 %copy-start.4 = (bf16[128,448]{0,1:T(8,128)(2,1)S(1)}, bf16[128,448]{0,1:T(8,128)(2,1)}, u32[]{:S(2)}) copy-start(bf16[128,448]{0,1:T(8,128)(2,1)} %param.17) | copy-start | bytes 344068
  23.4 98.7 %reduce-scatter.10.cloned.1.call-start = ((), (), s32[]{:S(2)}) async-start(), calls=%async_computation.7 | async-start | bytes 1179648
  89.5 123.9 %all-gather.6.cloned.1.call-start = ((), (), s32[]{:S(2)}) async-start(), calls=%async_computation.4 | async-start | bytes 1949696 | tf_op jit(solution)/shard_map/all_gather | solution.py:60
  167.3 200.0 %all-gather.8.cloned.1.call-start = ((), (), s32[]{:S(2)}) async-start(), calls=%async_computation.5 | async-start | bytes 16515072 | tf_op jit(solution)/shard_map/all_gather | solution.py:61
  213.4 333.3 %reduce-scatter.12.cloned.1.call-start = ((), (), s32[]{:S(2)}) async-start(), calls=%async_computation.8 | async-start | bytes 16515072
  367.3 10.4 %copy-start.2 = (bf16[1024,7168]{0,1:T(8,128)(2,1)S(1)}, bf16[1024,7168]{0,1:T(8,128)(2,1)}, u32[]{:S(2)}) copy-start(bf16[1024,7168]{0,1:T(8,128)(2,1)} %all-gather.8.cloned.1.call-done) | copy-start | bytes 44040196
  367.3 11.4 %copy-start.8 = (bf16[1,7168,256]{2,1,0:T(8,128)(2,1)S(1)}, bf16[1,7168,256]{2,1,0:T(8,128)(2,1)}, u32[]{:S(2)}) copy-start(bf16[1,7168,256]{2,1,0:T(8,128)(2,1)} %param.22) | copy-start | bytes 11010052
  378.7 4.1 copy-start.3
  390.1 0.7 copy-start.5
  390.1 0.7 copy-start.6
  390.1 230.6 %reduce-scatter.8.cloned.1.call-start = ((), (), s32[]{:S(2)}) async-start(), calls=%async_computation.6 | async-start | bytes 1949696 | tf_op jit(solution)/shard_map/reduce_scatter | solution.py:72
  546.7 75.7 %copy-start.1 = (bf16[16,512,128]{2,1,0:T(8,128)(2,1)S(1)}, bf16[16,512,128]{2,1,0:T(8,128)(2,1)}, u32[]{:S(2)}) copy-start(bf16[16,512,128]{2,1,0:T(8,128)(2,1)} %param.15) | copy-start | bytes 6291460
Sparse Core Ops, SparseCore 0:
  23.5 59.7 all-gather.3
  89.6 32.4 reduce-scatter.9
  167.4 45.8 all-gather.5
  214.8 152.4 all-gather.7
  390.3 156.3 reduce-scatter.11
  554.0 66.7 reduce-scatter.7
where the time goes:
time: 631 us; the launch traced here: 629 us
  waiting for transfers between devices  515 us (82%)
  blocking collectives  43.3 us (7%)
  matrix products  39.6 us (6%)
  between operations  13.6 us (2%)
  local copies, waits for them, and re-layouts  10.7 us (2%)
  other arithmetic  6.82 us (1%)
    unnamed x8, waiting for transfers between devices  188 us
    all_gather x1, waiting for transfers between devices, shards(): row_piece = lax.all_gather(full_block, 'col', axis=0, tiled=True)  154 us
    reduce_scatter x1, waiting for transfers between devices, shards(): lax.psum_scatter(weighted.astype(jnp.bfloat16), ('side', 'row'), scatter_...  66.9 us
    all_gather x1, waiting for transfers between devices, shards(): lax.all_gather(head_out, ('side', 'row'), axis=0, tiled=True)  59.8 us
    all_gather x1, waiting for transfers between devices, shards(): full_block = lax.all_gather(normed, ('side', 'row'), axis=1, tiled=True)  46 us
    psum x1, blocking collectives, shards(): squares_total = lax.psum(jnp.sum(hidden * hidden, axis=1), ('side', 'row'))  43.3 us
  transfers between devices with their start and end apart: 6, of which 6 were waited for; matrix products, arithmetic and copies ran while one was open for 0% of the time, Pallas kernels for 0%

commit v1 on v0

v1 whole, which is shorter than its diff:
```python
import functools

import jax
import jax.numpy as jnp
from jax import lax
from jax.experimental import pallas as pl
from jax.experimental.pallas import tpu as pltpu
from jax.sharding import PartitionSpec as P

D = 7168
ROPE = 64
HD = 128
HALF = 64
PAIR = 896
MESH = pl.DeviceIdType.MESH
BF16 = jnp.bfloat16
F32 = jnp.float32

LANES = ((0, 384), (384, 256), (640, 256))
ORDERS = (("x", "y", "z"), ("y", "z", "x"), ("z", "x", "y"))
SIZES = {"x": (2, 2, 4), "y": (2, 4, 2), "z": (4, 4)}


def position():
    row, col = lax.axis_index("row"), lax.axis_index("col")
    return {"x": col % 4, "y": row % 4, "z": (row // 4) * 2 + col // 4}


def chip_id(at):
    return (lax.axis_index("side"), (at["z"] // 2) * 4 + at["y"], (at["z"] % 2) * 4 + at["x"])


def neighbour(here, axis, step):
    return chip_id({**here, axis: (here[axis] + step + 4) % 4})


def sibling_id():
    return (1 - lax.axis_index("side"), lax.axis_index("row"), lax.axis_index("col"))


def view(ref, at, rows, lanes, lead=()):
    index = [slice(None)] * 4
    if "x" in at:
        index[1] = at["x"]
    if "y" in at:
        index[3] = at["y"]
    if "z" in at:
        index[0], index[2] = at["z"] % 2, at["z"] // 2
    return ref.at[(*lead, *index, pl.ds(*rows), pl.ds(*lanes))]


def lead_shape(fixed):
    shape = []
    if "z" not in fixed:
        shape.append(2)
    if "x" not in fixed:
        shape.append(4)
    if "z" not in fixed:
        shape.append(2)
    if "y" not in fixed:
        shape.append(4)
    return tuple(shape)


def enter(peers):
    barrier = pltpu.get_barrier_semaphore()
    for peer in peers:
        pl.semaphore_signal(barrier, inc=1, device_id=peer, device_id_type=MESH)
    pl.semaphore_wait(barrier, len(peers))


def ring_peers(here):
    return [sibling_id()] + [neighbour(here, axis, step) for axis in "xyz" for step in (1, -1)]


LOW, HIGH, ALL = (0, 32), (32, 32), (0, 64)


def gather_kernel(
    hidden_ref, gain_ref, gates_ref, gate_hbm, up_hbm, act_ref,
    rows_buf, weights, squares, total, load_sem, sq_send, sq_recv, send_sem, recv_sem, sib_send, sib_recv,
):
    side = lax.axis_index("side")
    row = lax.axis_index("row")
    here = position()
    loads = []
    for which, source in enumerate((gate_hbm, up_hbm)):
        for core in range(2):
            loads.append(
                pltpu.make_async_copy(
                    source.at[core],
                    weights.at[:, core, :, pl.ds(which * 256, 256)],
                    load_sem.at[which * 2 + core],
                )
            )
    for load in loads:
        load.start()
    row_peers = []
    for k in range(1, 8):
        other = (row + k) % 8
        row_peers.append((side, other, lax.axis_index("col")))
    enter(ring_peers(here) + row_peers)

    hidden = hidden_ref[...]
    squares[row] = jnp.broadcast_to(jnp.sum(hidden * hidden, axis=1, keepdims=True), (HALF, 128))
    copies = []
    for k in range(1, 8):
        copy = pltpu.make_async_remote_copy(
            src_ref=squares.at[row],
            dst_ref=squares.at[row],
            send_sem=sq_send.at[k],
            recv_sem=sq_recv.at[k],
            device_id=row_peers[k - 1],
            device_id_type=MESH,
        )
        copy.start()
        copies.append(copy)
    for copy in copies:
        copy.wait()
    sums = squares[0]
    for k in range(1, 8):
        sums = sums + squares[k]
    inverse = lax.rsqrt(sums[:, :1] / D + 1e-06)
    rows_buf[side, here["z"] % 2, here["x"], here["z"] // 2, here["y"]] = (
        hidden * inverse * gain_ref[...]
    ).astype(BF16)

    def ring_copy(part, phase, direction, piece, at, rows):
        axis = ORDERS[part][phase]
        ref = view(rows_buf, at, rows, LANES[part], (side,))
        return pltpu.make_async_remote_copy(
            src_ref=ref,
            dst_ref=ref,
            send_sem=send_sem.at[part, phase, direction, piece],
            recv_sem=recv_sem.at[part, phase, direction, piece],
            device_id=neighbour(here, axis, 1 - 2 * direction),
            device_id_type=MESH,
        )

    def share(part, index, at):
        ref = view(rows_buf, at, ALL, LANES[part], (side,))
        return pltpu.make_async_remote_copy(
            src_ref=ref,
            dst_ref=ref,
            send_sem=sib_send.at[part, index],
            recv_sem=sib_recv.at[part, index],
            device_id=sibling_id(),
            device_id_type=MESH,
        )

    sent, shared = [], []
    for phase in range(3):
        started = {}
        for part in range(3):
            axis = ORDERS[part][phase]
            own = {a: here[a] for a in ORDERS[part][phase:]}
            for direction, halves in enumerate(((LOW, HIGH), (HIGH, LOW))):
                for piece in range(2):
                    copy = ring_copy(part, phase, direction, piece, own, halves[piece])
                    copy.start()
                    started[part, direction, piece] = copy
            if phase == 2:
                copy = share(part, 0, own)
                copy.start()
                shared.append(copy)
        for part in range(3):
            axis = ORDERS[part][phase]
            own = {a: here[a] for a in ORDERS[part][phase:]}
            for direction, half in enumerate((LOW, HIGH)):
                step = 1 - 2 * direction
                started[part, direction, 0].wait_recv()
                source = {**own, axis: (here[axis] - step + 4) % 4}
                copy = ring_copy(part, phase, direction, 2, source, half)
                copy.start()
                started[part, direction, 2] = copy
        for part in range(3):
            axis = ORDERS[part][phase]
            own = {a: here[a] for a in ORDERS[part][phase:]}
            for direction in range(2):
                step = 1 - 2 * direction
                started[part, direction, 1].wait_recv()
                if phase == 2:
                    copy = share(part, 1 + direction, {**own, axis: (here[axis] - step + 4) % 4})
                    copy.start()
                    shared.append(copy)
        for part in range(3):
            axis = ORDERS[part][phase]
            own = {a: here[a] for a in ORDERS[part][phase:]}
            for direction in range(2):
                started[part, direction, 2].wait_recv()
            if phase == 2:
                copy = share(part, 3, {**own, axis: (here[axis] + 2) % 4})
                copy.start()
                shared.append(copy)
        sent += list(started.values())

    for load in loads:
        load.wait()

    def experts(half):
        total[...] = jnp.zeros_like(total)

        @pl.loop(0, 8)
        def _(r):
            lhs = rows_buf[half, :, :, r // 4, r % 4].reshape(8 * HALF, PAIR)
            total[...] += jnp.dot(lhs, weights[r].reshape(PAIR, 512), preferred_element_type=F32)

        gate_part = total[:, :256]
        value = gate_part / (1.0 + jnp.exp(-gate_part)) * total[:, 256:]
        act_ref[half] = (value * gates_ref[half]).astype(BF16)

    experts(side)
    for copy in shared:
        copy.wait_recv()
    experts(1 - side)
    for copy in sent + shared:
        copy.wait_send()


def scatter_kernel(
    act_ref, down_ref, hidden_ref, out_ref,
    stage, from_sibling, sums, mixed, mixed_sibling, *rest,
):
    arrivals, (sib_send, sib_recv, send_sem, recv_sem, out_send, out_recv) = rest[:9], rest[9:]
    side = lax.axis_index("side")
    here = position()
    enter(ring_peers(here))

    def sibling_copy(r):
        return pltpu.make_async_remote_copy(
            src_ref=stage.at[r],
            dst_ref=from_sibling.at[r],
            send_sem=sib_send.at[r],
            recv_sem=sib_recv.at[r],
            device_id=sibling_id(),
            device_id_type=MESH,
        )

    @pl.loop(0, 8)
    def _(r):
        stage[r] = jnp.dot(act_ref[1 - side], down_ref[r], preferred_element_type=F32).astype(BF16)
        sibling_copy(r).start()

    @pl.loop(0, 8)
    def _(r):
        own = jnp.dot(act_ref[side], down_ref[r], preferred_element_type=F32)
        sibling_copy(r).wait_recv()
        both = own + from_sibling[r].astype(F32)
        sums[:, :, r // 4, r % 4] = both.astype(BF16).reshape(2, 4, HALF, PAIR)

    def ring_copy(part, phase, direction, piece, at, rows):
        axis = ORDERS[part][phase]
        return pltpu.make_async_remote_copy(
            src_ref=view(sums, at, rows, LANES[part]),
            dst_ref=arrivals[part * 3 + phase].at[direction, piece],
            send_sem=send_sem.at[part, phase, direction, piece],
            recv_sem=recv_sem.at[part, phase, direction, piece],
            device_id=neighbour(here, axis, 1 - 2 * direction),
            device_id_type=MESH,
        )

    sent = []
    for phase in range(3):
        started = {}
        for part in range(3):
            axis = ORDERS[part][phase]
            done = {a: here[a] for a in ORDERS[part][:phase]}
            far = {**done, axis: (here[axis] + 2) % 4}
            for direction, (through, direct) in enumerate(((LOW, HIGH), (HIGH, LOW))):
                step = 1 - 2 * direction
                near = {**done, axis: (here[axis] + step + 4) % 4}
                for piece, (at, rows) in enumerate(((far, through), (near, direct))):
                    copy = ring_copy(part, phase, direction, piece, at, rows)
                    copy.start()
                    started[part, direction, piece] = copy
        for part in range(3):
            axis = ORDERS[part][phase]
            done = {a: here[a] for a in ORDERS[part][:phase]}
            arrived = arrivals[part * 3 + phase]
            for direction, through in enumerate((LOW, HIGH)):
                step = 1 - 2 * direction
                near = {**done, axis: (here[axis] + step + 4) % 4}
                started[part, direction, 0].wait_recv()
                target = view(sums, near, through, LANES[part])
                target[...] = (target[...].astype(F32) + arrived[direction, 0].astype(F32)).astype(BF16)
                copy = ring_copy(part, phase, direction, 2, near, through)
                copy.start()
                started[part, direction, 2] = copy
        for part in range(3):
            axis = ORDERS[part][phase]
            own = {a: here[a] for a in ORDERS[part][: phase + 1]}
            arrived = arrivals[part * 3 + phase]
            for direction in range(2):
                started[part, direction, 1].wait_recv()
                started[part, direction, 2].wait_recv()
            for rows, (first, second) in ((LOW, (2, 1)), (HIGH, (1, 2))):
                target = view(sums, own, rows, LANES[part])
                value = target[...].astype(F32) + (
                    arrived[0, first].astype(F32) + arrived[1, second].astype(F32)
                )
                if phase < 2:
                    target[...] = value.astype(BF16)
                else:
                    spot = (pl.ds(*rows), pl.ds(*LANES[part]))
                    mixed[spot] = (hidden_ref[spot] + value).astype(BF16)
        sent += list(started.values())

    copy = pltpu.make_async_remote_copy(
        src_ref=mixed,
        dst_ref=mixed_sibling,
        send_sem=out_send,
        recv_sem=out_recv,
        device_id=sibling_id(),
        device_id_type=MESH,
    )
    copy.start()
    copy.wait_recv()

    @pl.when(side == 0)
    def _():
        out_ref[0:64] = mixed[:, 0:448]
        out_ref[64:128] = mixed_sibling[:, 0:448]

    @pl.when(side == 1)
    def _():
        out_ref[0:64] = mixed_sibling[:, 448:896]
        out_ref[64:128] = mixed[:, 448:896]

    copy.wait_send()
    for copy in sent:
        copy.wait_send()

    @pl.loop(0, 8)
    def _(r):
        sibling_copy(r).wait_send()


VMEM = pl.BlockSpec(memory_space=pltpu.VMEM)
ANY = pl.BlockSpec(memory_space=pl.ANY)


def gather_call(hidden, gain, gates, w_gate, w_up):
    return pl.pallas_call(
        gather_kernel,
        out_shape=jax.ShapeDtypeStruct((2, 8 * HALF, 256), BF16),
        in_specs=[VMEM, VMEM, VMEM, ANY, ANY],
        out_specs=VMEM,
        scratch_shapes=[
            pltpu.VMEM((2, 2, 4, 2, 4, HALF, PAIR), BF16),
            pltpu.VMEM((8, 2, 448, 512), BF16),
            pltpu.VMEM((8, HALF, 128), F32),
            pltpu.VMEM((8 * HALF, 512), F32),
            pltpu.SemaphoreType.DMA((4,)),
            pltpu.SemaphoreType.DMA((8,)),
            pltpu.SemaphoreType.DMA((8,)),
            pltpu.SemaphoreType.DMA((3, 3, 2, 3)),
            pltpu.SemaphoreType.DMA((3, 3, 2, 3)),
            pltpu.SemaphoreType.DMA((3, 4)),
            pltpu.SemaphoreType.DMA((3, 4)),
        ],
        compiler_params=pltpu.CompilerParams(
            collective_id=0, has_side_effects=True, vmem_limit_bytes=48 * 2**20
        ),
        cost_estimate=pl.CostEstimate(
            flops=2 * 1024 * 7168 * 512, bytes_accessed=8 * 2**20, transcendentals=2**18
        ),
    )(hidden, gain, gates, w_gate, w_up)


def scatter_call(act, down, hidden):
    arrivals = []
    for part in range(3):
        for phase in range(3):
            fixed = ORDERS[part][: phase + 1]
            arrivals.append(pltpu.VMEM((2, 3, *lead_shape(fixed), 32, LANES[part][1]), BF16))
    return pl.pallas_call(
        scatter_kernel,
        out_shape=jax.ShapeDtypeStruct((2 * HALF, 448), BF16),
        in_specs=[VMEM, VMEM, VMEM],
        out_specs=VMEM,
        scratch_shapes=[
            pltpu.VMEM((8, 8 * HALF, PAIR), BF16),
            pltpu.VMEM((8, 8 * HALF, PAIR), BF16),
            pltpu.VMEM((2, 4, 2, 4, HALF, PAIR), BF16),
            pltpu.VMEM((HALF, PAIR), BF16),
            pltpu.VMEM((HALF, PAIR), BF16),
            *arrivals,
            pltpu.SemaphoreType.DMA((8,)),
            pltpu.SemaphoreType.DMA((8,)),
            pltpu.SemaphoreType.DMA((3, 3, 2, 3)),
            pltpu.SemaphoreType.DMA((3, 3, 2, 3)),
            pltpu.SemaphoreType.DMA,
            pltpu.SemaphoreType.DMA,
        ],
        compiler_params=pltpu.CompilerParams(
            collective_id=1, has_side_effects=True, vmem_limit_bytes=52 * 2**20
        ),
        cost_estimate=pl.CostEstimate(
            flops=2 * 1024 * 7168 * 256, bytes_accessed=4 * 2**20, transcendentals=0
        ),
    )(act, down, hidden)


def shards(
    queries,
    cache,
    lengths,
    w_uv,
    w_out,
    residual_in,
    norm_gain,
    expert_ids,
    gate_vals,
    w_gate,
    w_up,
    w_down,
):
    side = lax.axis_index("side")
    owner_index = lax.axis_index(("side", "row"))
    my_gate = jnp.sum(jnp.where(expert_ids == owner_index, gate_vals, 0.0), axis=1)
    gates = lax.all_gather(my_gate, "col", axis=0, tiled=True)
    gates = gates.reshape(8, 2, HALF).transpose(1, 0, 2).reshape(2, 8 * HALF, 1)
    pair_out = lax.all_gather(w_out, "side", axis=1, tiled=True)
    pair_residual = lax.all_gather(residual_in, "side", axis=1, tiled=True)
    pair_gain = lax.all_gather(norm_gain, "side", axis=0, tiled=True)

    score_scale = (HD + ROPE) ** (-0.5)
    scores = (
        jnp.einsum("rhk,rlk->rhl", queries, cache, preferred_element_type=jnp.float32) * score_scale
    )
    places = lax.broadcasted_iota(jnp.int32, (1, 1, cache.shape[1]), 2)
    scores = jnp.where(places < lengths[:, None, None], scores, -jnp.inf)
    row_top = jnp.max(scores, axis=2, keepdims=True)
    exp_terms = jnp.exp(scores - row_top)
    attn_probs = (exp_terms / jnp.sum(exp_terms, axis=2, keepdims=True)).astype(jnp.bfloat16)
    latent_width = w_uv.shape[1]
    latent = jnp.einsum(
        "rhl,rlk->rhk", attn_probs, cache[:, :, :latent_width], preferred_element_type=jnp.float32
    ).astype(jnp.bfloat16)
    head_out = jnp.einsum("rhk,hkd->rhd", latent, w_uv, preferred_element_type=jnp.float32).astype(
        jnp.bfloat16
    )
    head_out = head_out.reshape(head_out.shape[0], -1)
    all_heads = lax.all_gather(head_out, ("side", "row"), axis=0, tiled=True)
    half_heads = lax.dynamic_index_in_dim(all_heads.reshape(8, 2, HALF, -1), side, 1, keepdims=False)
    partial_rows = jnp.dot(half_heads.reshape(8 * HALF, -1), pair_out, preferred_element_type=jnp.float32)
    attn_slice = lax.psum_scatter(
        partial_rows.astype(jnp.bfloat16), "col", scatter_dimension=0, tiled=True
    ).astype(jnp.float32)
    half_residual = lax.dynamic_slice_in_dim(pair_residual, side * HALF, HALF, 0)
    hidden = half_residual.astype(jnp.float32) + attn_slice
    act = gather_call(
        hidden,
        pair_gain.astype(jnp.float32).reshape(1, PAIR),
        gates,
        w_gate.reshape(2, 8, 448, 256),
        w_up.reshape(2, 8, 448, 256),
    )
    down = w_down.reshape(256, 2, 8, 448).transpose(2, 0, 1, 3).reshape(8, 256, PAIR)
    return scatter_call(act, down, hidden)


def solution(mesh):
    placed = (
        P(("side", "row"), "col", None),
        P(("side", "row"), None, None),
        P(("side", "row")),
        P("col", None, None),
        P("col", ("side", "row")),
        P("col", ("side", "row")),
        P(("side", "row")),
        P("col", None),
        P("col", None),
        P(("side", "row"), None, "col"),
        P(("side", "row"), None, "col"),
        P(("side", "row"), "col", None),
    )
    return jax.shard_map(
        shards, mesh=mesh, in_specs=placed, out_specs=P("col", ("side", "row")), check_vma=False
    )
```

time: 631 us -> 288 us (0.46)
  waiting for transfers between devices: 515 us -> 72.5 us
  Pallas kernels: 0 us -> 128 us
  blocking collectives: 43.3 us -> 23.2 us
  matrix products: 39.6 us -> 20.9 us
  local copies, waits for them, and re-layouts: 10.7 us -> 25.3 us
    unnamed x8 -> x3, waiting for transfers between devices: 188 us -> 0.73 us
    all_gather x3 -> x2, waiting for transfers between devices: 259 us -> 71.8 us  [the longest x1 59.1 us: shards(): all_heads = lax.all_gather(head_out, ('side', 'row'), axis=0, tiled=True)]
    pallas_call x0 -> x2, Pallas kernels: none -> 128 us  [the longest x1 64.2 us: scatter_call(): pl.pallas_call(scatter_kernel, out_shape=jax.ShapeDtypeStruct((2 * HALF,...]
    reduce_scatter x1, waiting for transfers between devices: 66.9 us -> 0.01 us  [shards(): lax.psum_scatter(partial_rows.astype(jnp.bfloat16), 'col', scatter_dimens...]
    psum x1 -> x0, blocking collectives: 43.3 us -> none  [shards(): squares_total = lax.psum(jnp.sum(hidden * hidden, axis=1), ('side', 'row'))]
    dot_general x4 -> x1, matrix products: 24.7 us -> 6.02 us  [shards(): jnp.dot(half_heads.reshape(8 * HALF, -1), pair_out, preferred_element_typ...]
    all_gather x0 -> x2, blocking collectives: none -> 17.4 us  [the longest x1 15.4 us: shards(): gates = lax.all_gather(my_gate, 'col', axis=0, tiled=True)]
    reshape x0 -> x5, local copies, waits for them, and re-layouts: none -> 6.79 us  [the longest x1 6.23 us: shards(): w_down.reshape(256, 2, 8, 448).transpose(2, 0, 1, 3).reshape(8, 256, PAIR)]
  transfers between devices with their start and end apart: 6 -> 3, of which waited for: 6 -> 2; matrix products, arithmetic and copies ran while one was open for 0% -> 8% of each run, Pallas kernels for 0% -> 0%
where the time goes in v1:
time: 288 us; the launch traced here: 287 us
  Pallas kernels  128 us (44%)
  waiting for transfers between devices  72.5 us (25%)
  local copies, waits for them, and re-layouts  25.3 us (9%)
  blocking collectives  23.2 us (8%)
  matrix products  20.9 us (7%)
  between operations  13.9 us (5%)
    pallas_call x1, Pallas kernels, scatter_call(): pl.pallas_call(scatter_kernel, out_shape=jax.ShapeDtypeStruct((2 * HALF,...  64.2 us
    pallas_call x1, Pallas kernels, gather_call(): pl.pallas_call(gather_kernel, out_shape=jax.ShapeDtypeStruct((2, 8 * HALF...  63.9 us
    all_gather x1, waiting for transfers between devices, shards(): all_heads = lax.all_gather(head_out, ('side', 'row'), axis=0, tiled=True)  59.1 us
    all_gather x1, blocking collectives, shards(): gates = lax.all_gather(my_gate, 'col', axis=0, tiled=True)  15.4 us
    all_gather x1, waiting for transfers between devices, shards(): pair_out = lax.all_gather(w_out, 'side', axis=1, tiled=True)  12.7 us
    unnamed x19, local copies, waits for them, and re-layouts  8.94 us
    dot_general x1, matrix products, shards(): jnp.einsum('rhl,rlk->rhk', attn_probs, cache[:, :, :latent_width], prefer...  6.73 us
    reshape x1, local copies, waits for them, and re-layouts, shards(): w_down.reshape(256, 2, 8, 448).transpose(2, 0, 1, 3).reshape(8, 256, PAIR)  6.23 us
  transfers between devices with their start and end apart: 3, of which 2 were waited for; matrix products, arithmetic and copies ran while one was open for 8% of the time, Pallas kernels for 0%

profile of v1, /device:TPU:1, one launch (start us, length us, event | category | flops | bytes accessed | tf_op | source)
XLA Modules:
  0.0 286.9 jit_solution(5126948234391462183)
XLA Ops:
  6.5 0.0 copy-start
  6.5 0.0 all-gather.4.cloned.1.call-start
  6.5 0.9 iota_compare_fusion
  7.4 5.6 %fusion.7 = f32[64,16,128]{2,1,0:T(8,128)S(1)} fusion(bf16[64,16,576]{2,1,0:T(8,128)(2,1)} %param.12, bf16[64,128,576]{1,2,0:T(8,128)(2,1)} %param.13, pred[64,128]{1,0:T(8,128)(4,1)S(1)} %iota_compare_fusion), kind=kOutput, calls=%fused_computation.7 | convolution fusion | flops 151257088 | bytes 11149312 | tf_op jit(solution)/shard_map/rhk,rlk->rhl/dot_general | solution.py:429
  13.0 0.3 fusion.13
  13.4 6.7 %fusion.3 = bf16[64,16,512]{2,1,0:T(8,128)(2,1)} fusion(bf16[64,128,576]{1,2,0:T(8,128)(2,1)} %param.13, f32[64,16]{1,0:T(8,128)S(1)} %fusion.13, f32[64,16,128]{2,1,0:T(8,128)S(1)} %fusion.7), kind=kOutput, calls=%fused_computation.3 | convolution fusion | flops 135136384 | bytes 10518528 | tf_op jit(solution)/shard_map/rhl,rlk->rhk/dot_general | solution.py:437
  20.1 0.0 copy-done
  20.1 2.5 fusion.9
  22.6 0.8 copy.42
  23.4 0.0 all-gather.4.cloned.1.call-update
  23.4 0.0 all-gather.6.cloned.1.call-start
  23.5 0.7 all-gather.6.cloned.1.call-update
  24.2 0.0 reduce-scatter.2.cloned.1.call-start
  24.2 59.1 %all-gather.4.cloned.1.call-done = bf16[1024,2048]{1,0:T(8,128)(2,1)} async-done(((bf16[64,2048]{1,0:T(8,128)(2,1)}), bf16[1024,2048]{1,0:T(8,128)(2,1)}) %all-gather.4.cloned.1.call-update) | async-done | bytes 4194320 | tf_op jit(solution)/shard_map/all_gather | solution.py:444
  83.3 3.2 %constant_dynamic-slice_fusion = bf16[8,1,64,2048]{3,2,1,0:T(8,128)(2,1)} fusion(bf16[8,2,64,2048]{3,2,1,0:T(8,128)(2,1)} %bitcast.30, s32[]{:T(128)S(6)} %select_n.17), kind=kLoop, calls=%fused_computation.19 | loop fusion | bytes 4194308 | tf_op jit(solution)/shard_map/jit(dynamic_index_in_dim)/dynamic_slice | solution.py:445
  86.5 12.7 %all-gather.6.cloned.1.call-done = bf16[2048,896]{0,1:T(8,128)(2,1)} async-done(((bf16[2048,448]{0,1:T(8,128)(2,1)}), bf16[2048,896]{0,1:T(8,128)(2,1)}) %all-gather.6.cloned.1.call-update) | async-done | bytes 3670032 | tf_op jit(solution)/shard_map/all_gather | solution.py:423
  99.2 0.0 copy-start.2
  99.2 0.0 copy-start.3
  99.2 0.0 copy-start.4
  99.2 0.0 copy-start.6
  99.2 0.0 copy-start.5
  99.2 6.0 %convolution_convert_fusion = bf16[512,896]{1,0:T(8,128)(2,1)} fusion(bf16[512,2048]{1,0:T(8,128)(2,1)} %bitcast.29, bf16[2048,896]{0,1:T(8,128)(2,1)} %all-gather.6.cloned.1.call-done), kind=kOutput, calls=%fused_computation.4 | convolution fusion | flops 1879506944 | bytes 6684672 | tf_op jit(solution)/shard_map/dot_general | solution.py:446
  105.2 0.0 reduce-scatter.2.cloned.1.call-update
  105.3 0.0 copy-done.2
  105.3 2.0 all_gather.15
  107.3 0.1 constant_dynamic-slice_fusion.1
  107.4 0.1 copy.35
  107.5 0.0 copy-done.3
  107.6 0.0 copy-done.4
  107.6 15.4 %all-gather = f32[8,1,128]{2,1,0:T(1,128)S(1)} all-gather(f32[1,1,128]{2,1,0:T(1,128)S(1)} %bitcast.33), channel_id=1, replica_groups=mesh['side'=2,'row'=8,'col'=8] {'col'}, dimensions={0}, use_global_device_ids=true | all-gather | bytes 4608 | tf_op jit(solution)/shard_map/all_gather | solution.py:421
  123.0 0.5 broadcast.19
  123.5 0.7 reduce.3
  124.2 0.1 reshape.61
  124.2 0.5 reshape.77.gates_ref
  124.7 0.0 copy-done.6
  124.7 0.6 dynamic-slice
  126.0 0.0 copy-done.5
  126.0 0.2 dynamic-update-slice
  126.2 5.9 %all-reduce = bf16[896]{0:T(1024)(128)(2,1)S(1)} all-reduce(bf16[896]{0:T(1024)(128)(2,1)S(1)} %dynamic-update-slice), channel_id=1, replica_groups=mesh['side'=2,'row'=8,'col'=8] {'side'}, use_global_device_ids=true, to_apply=%add | all-reduce | flops 896 | bytes 3584
  132.1 5.9 %copy.31 = bf16[1,256,7168]{1,2,0:T(8,128)(2,1)} copy(bf16[1,256,7168]{2,1,0:T(8,128)(2,1)} %param.23) | data formatting | bytes 7340032 | tf_op args[11]
  138.0 4.2 %copy.32 = bf16[8,256,2,448]{1,3,2,0:T(8,128)(2,1)} copy(bf16[8,256,2,448]{1,3,0,2:T(8,128)(2,1)} %bitcast.28) | data formatting | bytes 7340032 | tf_op jit(solution)/shard_map/transpose | solution.py:459
  142.2 6.2 %copy.33.down_ref = bf16[8,256,896]{2,1,0:T(8,128)(2,1)} copy(bf16[8,256,896]{1,2,0:T(8,128)(2,1)} %bitcast.27) | data formatting | bytes 7340032 | tf_op jit(solution)/shard_map/reshape | solution.py:459
  148.5 0.9 convert_add_fusion.hidden_ref
  149.4 0.0 copy-start.1
  149.4 2.0 copy-done.1
  151.4 63.9 %shard_map.118.act_ref = bf16[2,512,256]{2,1,0:T(8,128)(2,1)S(1)} custom-call(f32[64,896]{1,0:T(8,128)S(1)} %convert_add_fusion.hidden_ref, f32[1,896]{1,0:T(1,128)S(1)} %reshape.68.gain_ref, f32[2,512,1]{2,1,0:T(8,128)S(1)} %reshape.77.gates_ref, bf16[2,8,448,256]{3,2,1,0:T(8,128)(2,1)S(1)} %bitcast.26, bf16[2,8,448,256]{3,2,1,0:T(8,128)(2,1)} %bitcast.34), custom_call_target="tpu_custom_call" | custom-call | flops 7516192768 | bytes 8388608 | tf_op jit(solution)/shard_map/pallas_call | solution.py:343
  215.4 64.2 %shard_map.119 = bf16[128,448]{1,0:T(8,128)(2,1)S(1)} custom-call(bf16[2,512,256]{2,1,0:T(8,128)(2,1)S(1)} %shard_map.118.act_ref, bf16[8,256,896]{2,1,0:T(8,128)(2,1)} %copy.33.down_ref, f32[64,896]{1,0:T(8,128)S(1)} %convert_add_fusion.hidden_ref), custom_call_target="tpu_custom_call" | custom-call | flops 3758096384 | bytes 4194304 | tf_op jit(solution)/shard_map/pallas_call | solution.py:376
  279.6 0.8 copy.34
  (5 shorter events, 0.0 us)
Async XLA Ops:
  6.5 13.6 %copy-start = (bf16[16,512,128]{2,1,0:T(8,128)(2,1)S(1)}, bf16[16,512,128]{2,1,0:T(8,128)(2,1)}, u32[]{:S(2)}) copy-start(bf16[16,512,128]{2,1,0:T(8,128)(2,1)} %param.15) | copy-start | bytes 6291460
  6.5 76.8 %all-gather.4.cloned.1.call-start = ((), (), s32[]{:S(2)}) async-start(), calls=%async_computation.1 | async-start | bytes 4456448 | tf_op jit(solution)/shard_map/all_gather | solution.py:444
  23.4 75.8 %all-gather.6.cloned.1.call-start = ((), (), s32[]{:S(2)}) async-start(), calls=%async_computation.2 | async-start | bytes 5505024 | tf_op jit(solution)/shard_map/all_gather | solution.py:423
  24.2 124.3 %reduce-scatter.2.cloned.1.call-start = ((), (), s32[]{:S(2)}) async-start(), calls=%async_computation.3 | async-start | bytes 1032192 | tf_op jit(solution)/shard_map/reduce_scatter | solution.py:447
  99.2 6.1 %copy-start.2 = (bf16[128,448]{0,1:T(8,128)(2,1)S(1)}, bf16[128,448]{0,1:T(8,128)(2,1)}, u32[]{:S(2)}) copy-start(bf16[128,448]{0,1:T(8,128)(2,1)} %param.17) | copy-start | bytes 344068
  99.2 8.3 %copy-start.3 = (f32[128,8]{0,1:T(8,128)S(1)}, f32[128,8]{0,1:T(8,128)}, u32[]{:S(2)}) copy-start(f32[128,8]{0,1:T(8,128)} %param.20) | copy-start | bytes 12292
  99.2 8.3 %copy-start.4 = (s32[128,8]{0,1:T(8,128)S(1)}, s32[128,8]{0,1:T(8,128)}, u32[]{:S(2)}) copy-start(s32[128,8]{0,1:T(8,128)} %param.19) | copy-start | bytes 12292
  99.2 25.5 %copy-start.6 = (u32[128]{0:T(128)S(1)}, u32[128]{0:T(128)}, u32[]{:S(2)}) copy-start(u32[128]{0:T(128)} %constant.35) | copy-start | bytes 1540
  99.2 26.8 %copy-start.5 = (bf16[448]{0:T(512)(128)(2,1)S(1)}, bf16[448]{0:T(512)(128)(2,1)}, u32[]{:S(2)}) copy-start(bf16[448]{0:T(512)(128)(2,1)} %param.18) | copy-start | bytes 2692
  149.4 2.0 copy-start.1
Sparse Core Ops, SparseCore 0:
  23.5 59.7 all-gather.3
  84.9 14.2 all-gather.5
  105.4 34.7 reduce-scatter.1

commit v2 on v0

v2 whole, which is shorter than its diff:
```python
import jax
import jax.numpy as jnp
from jax import lax
from jax.experimental import pallas as pl
from jax.experimental.pallas import tpu as pltpu
from jax.sharding import PartitionSpec as P

D = 7168
ROPE = 64
HD = 128
HALF = 64
OWN = 448
PAIR = 896
MESH = pl.DeviceIdType.MESH
BF16 = jnp.bfloat16
F32 = jnp.float32

LANES = ((0, 384), (384, 256), (640, 256))
ORDERS = (
    (("x", "y", "z"), ("y", "z", "x"), ("z", "x", "y")),
    (("y", "z", "x"), ("z", "x", "y"), ("x", "y", "z")),
)
HEAD_LANES = ((0, 1152), (1152, 896))
SUM_LANES = ((0, 512), (512, 384))
LOW, HIGH, ALL = (0, 32), (32, 32), (0, 64)


def position():
    row, col = lax.axis_index("row"), lax.axis_index("col")
    return {"x": col % 4, "y": row % 4, "z": (row // 4) * 2 + col // 4}


def chip_id(at):
    return (lax.axis_index("side"), (at["z"] // 2) * 4 + at["y"], (at["z"] % 2) * 4 + at["x"])


def neighbour(here, axis, step):
    return chip_id({**here, axis: (here[axis] + step + 4) % 4})


def sibling_id():
    return (1 - lax.axis_index("side"), lax.axis_index("row"), lax.axis_index("col"))


def view(ref, at, rows, lanes, lead=()):
    index = [slice(None)] * 6
    if "x" in at:
        index[1], index[2] = at["x"] // 2, at["x"] % 2
    if "y" in at:
        index[4], index[5] = at["y"] // 2, at["y"] % 2
    if "z" in at:
        index[0], index[3] = at["z"] % 2, at["z"] // 2
    return ref.at[(*lead, *index, pl.ds(*rows), pl.ds(*lanes))]


def remote(src, dst, send_sem, recv_sem, device):
    return pltpu.make_async_remote_copy(
        src_ref=src,
        dst_ref=dst,
        send_sem=send_sem,
        recv_sem=recv_sem,
        device_id=device,
        device_id_type=MESH,
    )


class RingGather:
    def __init__(self, here, axis, bundle, sems):
        self.here, self.axis, self.bundle, self.sems = here, axis, bundle, sems
        self.copies = {}

    def go(self, direction, piece, j, rows):
        send, recv = self.sems
        ref = self.bundle(j, rows)
        device = neighbour(self.here, self.axis, 1 - 2 * direction)
        copy = remote(ref, ref, send.at[direction, piece], recv.at[direction, piece], device)
        copy.start()
        self.copies[direction, piece] = copy

    def start(self):
        me = self.here[self.axis]
        for piece in range(2):
            for direction, halves in enumerate(((LOW, HIGH), (HIGH, LOW))):
                self.go(direction, piece, me, halves[piece])

    def relay(self):
        for direction, half in enumerate((LOW, HIGH)):
            self.copies[direction, 0].wait_recv()
            self.go(direction, 2, (self.here[self.axis] - 1 + 2 * direction + 4) % 4, half)

    def near(self):
        for direction in range(2):
            self.copies[direction, 1].wait_recv()

    def far(self):
        for direction in range(2):
            self.copies[direction, 2].wait_recv()

    def drain(self):
        for copy in self.copies.values():
            copy.wait_send()


class RingScatter:
    def __init__(self, here, axis, bundle, arrived, sems):
        self.here, self.axis, self.bundle, self.arrived, self.sems = here, axis, bundle, arrived, sems
        self.copies = {}

    def go(self, direction, piece, j, rows):
        send, recv = self.sems
        device = neighbour(self.here, self.axis, 1 - 2 * direction)
        copy = remote(
            self.bundle(j, rows),
            self.arrived.at[direction, piece],
            send.at[direction, piece],
            recv.at[direction, piece],
            device,
        )
        copy.start()
        self.copies[direction, piece] = copy

    def start(self):
        me = self.here[self.axis]
        for direction, half in enumerate((LOW, HIGH)):
            self.go(direction, 0, (me + 2) % 4, half)
        for direction, half in enumerate((HIGH, LOW)):
            self.go(direction, 1, (me + 1 - 2 * direction + 4) % 4, half)

    def relay(self):
        me = self.here[self.axis]
        for direction, half in enumerate((LOW, HIGH)):
            j = (me + 1 - 2 * direction + 4) % 4
            self.copies[direction, 0].wait_recv()
            target = self.bundle(j, half)
            target[...] = (target[...].astype(F32) + self.arrived[direction, 0].astype(F32)).astype(BF16)
            self.go(direction, 2, j, half)

    def finish(self, use=None):
        for direction in range(2):
            self.copies[direction, 1].wait_recv()
            self.copies[direction, 2].wait_recv()
        for rows, (first, second) in ((LOW, (2, 1)), (HIGH, (1, 2))):
            target = self.bundle(self.here[self.axis], rows)
            value = target[...].astype(F32) + (
                self.arrived[0, first].astype(F32) + self.arrived[1, second].astype(F32)
            )
            if use is None:
                target[...] = value.astype(BF16)
            else:
                use(rows, value)

    def drain(self):
        for copy in self.copies.values():
            copy.wait_send()


def layer_kernel(
    head_ref, pair_ref, gate_ref, out_hbm, gate_hbm, up_hbm, down_hbm, out_ref,
    heads, proj, part_sums, z_early, z_late, x_early, x_late, pair_sib, pair_all, hidden,
    rows_buf, weights, down, down_pairs, total, squares, inverses, gates, columns,
    from_sibling, mixed, mixed_sib,
    load_sems, head_sems, flip_sems, sum_sems, pair_sems, proj_sems, small_send, small_recv,
    send_sems, recv_sems, share_send, share_recv, back_send, back_recv, *arrivals,
):
    side, row, col = lax.axis_index("side"), lax.axis_index("row"), lax.axis_index("col")
    here = position()
    x, y, z_hi, z_lo = here["x"], here["y"], here["z"] // 2, here["z"] % 2
    far_z = (side, (row + 4) % 8, col)
    flip_z = (side, row, (col + 4) % 8)
    sibling = sibling_id()
    row_peers = [(side, (row + k) % 8, col) for k in range(1, 8)]
    col_peers = [(side, row, (col + k) % 8) for k in range(1, 8)]

    loads = [
        pltpu.make_async_copy(
            source.at[core],
            weights.at[:, core, :, pl.ds(which * 256, 256)],
            load_sems.at[which * 2 + core],
        )
        for which, source in enumerate((gate_hbm, up_hbm))
        for core in range(2)
    ]
    load_proj = pltpu.make_async_copy(out_hbm, proj.at[side], load_sems.at[4])
    load_down = pltpu.make_async_copy(down_hbm, down, load_sems.at[5])
    load_proj.start()
    for load in loads:
        load.start()
    load_down.start()
    heads[side, z_hi, y // 2, y % 2] = head_ref[...]
    gates[col] = gate_ref[...]

    barrier = pltpu.get_barrier_semaphore()
    peers = [sibling, *row_peers, *col_peers, neighbour(here, "z", 1), neighbour(here, "z", -1)]
    for peer in peers:
        pl.semaphore_signal(barrier, inc=1, device_id=peer, device_id_type=MESH)
    pl.semaphore_wait(barrier, len(peers))

    def head_view(which, at, rows):
        return heads.at[(side, *at, pl.ds(*rows), pl.ds(*HEAD_LANES[which]))]

    def head_sem(which):
        return head_sems.at[0, which], head_sems.at[1, which]

    first = head_view(0, (z_hi, y // 2, y % 2), ALL)
    flip_first = remote(first, first, flip_sems.at[0, 0], flip_sems.at[1, 0], far_z)
    flip_first.start()
    ring_first = RingGather(
        here, "y", lambda j, rows: head_view(1, (z_hi, j // 2, j % 2), rows), head_sem(0)
    )
    ring_first.start()
    pair_copy = remote(pair_ref.at[1 - side], pair_sib, pair_sems.at[0], pair_sems.at[1], sibling)
    pair_copy.start()
    proj_copy = remote(out_hbm, proj.at[side], proj_sems.at[0], proj_sems.at[1], sibling)
    proj_copy.start()
    gate_copies = [
        remote(gates.at[col], gates.at[col], small_send.at[0, k], small_recv.at[0, k], col_peers[k])
        for k in range(7)
    ]
    for copy in gate_copies:
        copy.start()
    flip_first.wait_recv()
    ring_second = RingGather(
        here, "y", lambda j, rows: head_view(0, (slice(None), j // 2, j % 2), rows), head_sem(1)
    )
    ring_second.start()
    ring_first.relay()
    ring_first.near()
    ring_first.far()
    second = head_view(1, (z_hi, slice(None), slice(None)), ALL)
    flip_second = remote(second, second, flip_sems.at[0, 1], flip_sems.at[1, 1], far_z)
    flip_second.start()

    pair_copy.wait_recv()

    @pl.when(side == 0)
    def _():
        pair_all[:, 0:OWN] = pair_ref[0]
        pair_all[:, OWN:PAIR] = pair_sib[...]

    @pl.when(side == 1)
    def _():
        pair_all[:, 0:OWN] = pair_sib[...]
        pair_all[:, OWN:PAIR] = pair_ref[1]

    ring_second.relay()
    ring_second.near()
    ring_second.far()
    flip_second.wait_recv()
    theirs = heads.at[side, :, :, 1 - side]
    head_share = remote(theirs, theirs, pair_sems.at[2], pair_sems.at[3], sibling)
    head_share.start()

    load_proj.wait()
    proj_copy.wait_recv()

    def project(source):
        lhs = heads[source, :, :, side].reshape(4 * HALF, 2048)
        for core in range(2):
            value = jnp.dot(lhs, proj[core], preferred_element_type=F32).astype(BF16)
            part_sums[source, :, :, core * OWN : (core + 1) * OWN] = value.reshape(4, HALF, OWN)

    project(side)
    head_share.wait_recv()
    project(1 - side)

    def sum_sem(which):
        return sum_sems.at[0, which], sum_sems.at[1, which]

    def x_ring(which, lead, arrived):
        return RingScatter(
            here,
            "x",
            lambda j, rows: part_sums.at[lead, j, pl.ds(*rows), pl.ds(*SUM_LANES[which])],
            arrived,
            sum_sem(which),
        )

    early_flip = remote(
        part_sums.at[1 - z_lo, :, :, pl.ds(*SUM_LANES[1])], z_early, flip_sems.at[0, 2], flip_sems.at[1, 2], flip_z
    )
    early_flip.start()
    early_ring = x_ring(0, slice(None), x_early)
    early_ring.start()
    early_ring.relay()
    early_flip.wait_recv()
    mine = part_sums.at[z_lo, :, :, pl.ds(*SUM_LANES[1])]
    mine[...] = (mine[...].astype(F32) + z_early[...].astype(F32)).astype(BF16)
    late_ring = x_ring(1, z_lo, x_late)
    late_ring.start()
    early_ring.finish()
    late_flip = remote(
        part_sums.at[1 - z_lo, x, :, pl.ds(*SUM_LANES[0])], z_late, flip_sems.at[0, 3], flip_sems.at[1, 3], flip_z
    )
    late_flip.start()
    late_ring.relay()
    late_flip.wait_recv()
    left = pl.ds(*SUM_LANES[0])
    hidden[:, left] = pair_all[0:HALF, left].astype(F32) + (
        part_sums[z_lo, x, :, left].astype(F32) + z_late[...].astype(F32)
    )

    def right(rows, value):
        spot = (pl.ds(*rows), pl.ds(*SUM_LANES[1]))
        hidden[spot] = pair_all[spot].astype(F32) + value

    late_ring.finish(right)
    rows_buf[side, z_lo, x // 2, x % 2, z_hi, y // 2, y % 2] = (hidden[...] * pair_all[HALF : HALF + 1].astype(F32)).astype(BF16)

    def small(kind, src, dst, k, peer):
        copy = remote(src, dst, small_send.at[kind, k], small_recv.at[kind, k], peer)
        copy.start()
        return copy

    def gather(orders):
        rings, shared = [], []

        def share(part, index, at):
            ref = view(rows_buf, at, ALL, LANES[part], (side,))
            copy = remote(ref, ref, share_send.at[part, index], share_recv.at[part, index], sibling)
            copy.start()
            shared.append(copy)

        square_copies, inverse_copies = [], []
        for phase in range(3):
            now = []
            for part in range(3):
                axis = orders[part][phase]
                own = {a: here[a] for a in orders[part][phase:]}
                bundle = lambda j, rows, part=part, own=own, axis=axis: view(
                    rows_buf, {**own, axis: j}, rows, LANES[part], (side,)
                )
                ring = RingGather(
                    here, axis, bundle, (send_sems.at[0, part, phase], recv_sems.at[0, part, phase])
                )
                ring.start()
                if phase == 2:
                    share(part, 0, own)
                now.append((part, axis, own, ring))
            if phase == 0:
                value = hidden[...]
                columns[0:HALF] = jnp.broadcast_to(
                    jnp.sum(value * value, axis=1, keepdims=True), (HALF, 128)
                )
                columns[HALF:128] = jnp.zeros((HALF, 128), F32)
                squares[row] = columns[...].T[0:8]
                for k in range(7):
                    square_copies.append(small(1, squares.at[row], squares.at[row], k, row_peers[k]))
            if phase == 1:
                for copy in square_copies:
                    copy.wait_recv()
                sums = squares[0]
                for k in range(1, 8):
                    sums = sums + squares[k]
                inverses[side, col] = lax.rsqrt(sums / D + 1e-06)
                for k in range(7):
                    place = inverses.at[side, col]
                    inverse_copies.append(small(2, place, place, k, col_peers[k]))
            if phase == 2:
                for copy in inverse_copies:
                    copy.wait_recv()
                place = inverses.at[side]
                inverse_share = remote(place, place, pair_sems.at[4], pair_sems.at[5], sibling)
                inverse_share.start()
            for part, axis, own, ring in now:
                ring.relay()
            if phase == 2:
                load_down.wait()
                for r in range(8):
                    for core in range(2):
                        down_pairs[r, :, core * OWN : (core + 1) * OWN] = down[
                            :, (core * 8 + r) * OWN : (core * 8 + r + 1) * OWN
                        ]
            for part, axis, own, ring in now:
                ring.near()
                if phase == 2:
                    share(part, 1, {**own, axis: (here[axis] + 3) % 4})
                    share(part, 2, {**own, axis: (here[axis] + 1) % 4})
            for part, axis, own, ring in now:
                ring.far()
                if phase == 2:
                    share(part, 3, {**own, axis: (here[axis] + 2) % 4})
                rings.append(ring)
        for copy in shared:
            copy.wait_recv()
        inverse_share.wait()
        for ring in rings:
            ring.drain()
        for copy in shared + square_copies + inverse_copies:
            copy.wait_send()

    for core in range(2):
        @pl.when(side == core)
        def _(core=core):
            gather(ORDERS[core])

    for copy in gate_copies:
        copy.wait()
    columns[...] = jnp.zeros_like(columns)
    for c in range(8):
        columns[c : c + 1] = gates[c, 0:1]
        columns[8 + c : 9 + c] = inverses[side, c, 0:1]
        columns[16 + c : 17 + c] = inverses[1 - side, c, 0:1]
    columns[...] = columns[...].T
    for load in loads:
        load.wait()

    def experts(half, place):
        total[...] = jnp.zeros_like(total)

        @pl.loop(0, 8)
        def _(r):
            lhs = rows_buf[half, :, :, :, r // 4, r // 2 % 2, r % 2].reshape(8 * HALF, PAIR)
            total[...] += jnp.dot(lhs, weights[r].reshape(PAIR, 512), preferred_element_type=F32)

        gate_rows = columns[pl.ds(pl.multiple_of(half * HALF, HALF), HALF), 0:8]
        scales = columns[0:HALF]
        acts = []
        for c in range(8):
            scale = scales[:, place + c : place + c + 1]
            gate_part = total[c * HALF : (c + 1) * HALF, :256] * scale
            up_part = total[c * HALF : (c + 1) * HALF, 256:] * (scale * gate_rows[:, c : c + 1])
            acts.append((gate_part / (1.0 + jnp.exp(-gate_part)) * up_part).astype(BF16))
        return jnp.concatenate(acts, axis=0)

    theirs_act = experts(1 - side, 16)

    def back(r):
        return remote(
            rows_buf.at[1 - side, :, :, :, r // 4, r // 2 % 2, r % 2],
            from_sibling.at[r],
            back_send.at[r],
            back_recv.at[r],
            sibling,
        )

    @pl.loop(0, 8)
    def _(r):
        value = jnp.dot(theirs_act, down_pairs[r], preferred_element_type=F32).astype(BF16)
        rows_buf[1 - side, :, :, :, r // 4, r // 2 % 2, r % 2] = value.reshape(2, 2, 2, HALF, PAIR)
        back(r).start()

    own_act = experts(side, 8)

    @pl.loop(0, 8)
    def _(r):
        value = jnp.dot(own_act, down_pairs[r], preferred_element_type=F32)
        back(r).wait_recv()
        value = value + from_sibling[r].reshape(8 * HALF, PAIR).astype(F32)
        rows_buf[side, :, :, :, r // 4, r // 2 % 2, r % 2] = value.astype(BF16).reshape(2, 2, 2, HALF, PAIR)

    def scatter(orders):
        rings = []
        for phase in range(3):
            now = []
            for part in range(3):
                axis = orders[part][phase]
                done = {a: here[a] for a in orders[part][:phase]}
                bundle = lambda j, rows, part=part, done=done, axis=axis: view(
                    rows_buf, {**done, axis: j}, rows, LANES[part], (side,)
                )
                ring = RingScatter(
                    here,
                    axis,
                    bundle,
                    arrivals[part * 3 + phase],
                    (send_sems.at[1, part, phase], recv_sems.at[1, part, phase]),
                )
                ring.start()
                now.append((part, ring))
            for part, ring in now:
                ring.relay()
            for part, ring in now:
                if phase < 2:
                    ring.finish()
                else:

                    def use(rows, value, part=part):
                        spot = (pl.ds(*rows), pl.ds(*LANES[part]))
                        mixed[spot] = (hidden[spot] + value).astype(BF16)

                    ring.finish(use)
                rings.append(ring)
        for ring in rings:
            ring.drain()

    for core in range(2):
        @pl.when(side == core)
        def _(core=core):
            scatter(ORDERS[core])

    last = remote(mixed, mixed_sib, pair_sems.at[6], pair_sems.at[7], sibling)
    last.start()
    last.wait_recv()

    @pl.when(side == 0)
    def _():
        out_ref[0:HALF] = mixed[:, 0:OWN]
        out_ref[HALF : 2 * HALF] = mixed_sib[:, 0:OWN]

    @pl.when(side == 1)
    def _():
        out_ref[0:HALF] = mixed_sib[:, OWN:PAIR]
        out_ref[HALF : 2 * HALF] = mixed[:, OWN:PAIR]

    last.wait_send()
    for ring in (ring_first, ring_second, early_ring, late_ring):
        ring.drain()
    for copy in (flip_first, flip_second, early_flip, late_flip, pair_copy, proj_copy, head_share):
        copy.wait_send()

    @pl.loop(0, 8)
    def _(r):
        back(r).wait_send()


ARRIVALS = [
    (2, 3, *(2,) * (4 - 2 * phase), 32, LANES[part][1]) for part in range(3) for phase in range(3)
]

VMEM = pl.BlockSpec(memory_space=pltpu.VMEM)
ANY = pl.BlockSpec(memory_space=pl.ANY)
DMA = pltpu.SemaphoreType.DMA


def layer_call(head_out, pair, gate_tile, w_out, w_gate, w_up, w_down):
    scratch = [
        pltpu.VMEM((2, 2, 2, 2, HALF, 2048), BF16),
        pltpu.VMEM((2, 2048, OWN), BF16),
        pltpu.VMEM((2, 4, HALF, PAIR), BF16),
        pltpu.VMEM((4, HALF, SUM_LANES[1][1]), BF16),
        pltpu.VMEM((HALF, SUM_LANES[0][1]), BF16),
        pltpu.VMEM((2, 3, 2, 32, SUM_LANES[0][1]), BF16),
        pltpu.VMEM((2, 3, 32, SUM_LANES[1][1]), BF16),
        pltpu.VMEM((80, OWN), BF16),
        pltpu.VMEM((80, PAIR), BF16),
        pltpu.VMEM((HALF, PAIR), F32),
        pltpu.VMEM((2, 2, 2, 2, 2, 2, 2, HALF, PAIR), BF16),
        pltpu.VMEM((8, 2, OWN, 512), BF16),
        pltpu.VMEM((256, D), BF16),
        pltpu.VMEM((8, 256, PAIR), BF16),
        pltpu.VMEM((8 * HALF, 512), F32),
        pltpu.VMEM((8, 8, 128), F32),
        pltpu.VMEM((2, 8, 8, 128), F32),
        pltpu.VMEM((8, 8, 128), F32),
        pltpu.VMEM((128, 128), F32),
        pltpu.VMEM((8, 2, 2, 2, HALF, PAIR), BF16),
        pltpu.VMEM((HALF, PAIR), BF16),
        pltpu.VMEM((HALF, PAIR), BF16),
        DMA((6,)),
        DMA((2, 2, 2, 3)),
        DMA((2, 4)),
        DMA((2, 2, 2, 3)),
        DMA((8,)),
        DMA((2,)),
        DMA((3, 7)),
        DMA((3, 7)),
        DMA((2, 3, 3, 2, 3)),
        DMA((2, 3, 3, 2, 3)),
        DMA((3, 4)),
        DMA((3, 4)),
        DMA((8,)),
        DMA((8,)),
        *[pltpu.VMEM(shape, BF16) for shape in ARRIVALS],
    ]
    return pl.pallas_call(
        layer_kernel,
        out_shape=jax.ShapeDtypeStruct((2 * HALF, OWN), BF16),
        in_specs=[VMEM, VMEM, VMEM, ANY, ANY, ANY, ANY],
        out_specs=VMEM,
        scratch_shapes=scratch,
        compiler_params=pltpu.CompilerParams(
            collective_id=0, has_side_effects=True, vmem_limit_bytes=58 * 2**20
        ),
        cost_estimate=pl.CostEstimate(
            flops=2 * 1024 * 7168 * 1000, bytes_accessed=16 * 2**20, transcendentals=2**18
        ),
    )(head_out, pair, gate_tile, w_out, w_gate, w_up, w_down)


def shards(
    queries,
    cache,
    lengths,
    w_uv,
    w_out,
    residual_in,
    norm_gain,
    expert_ids,
    gate_vals,
    w_gate,
    w_up,
    w_down,
):
    owner_index = lax.axis_index(("side", "row"))
    my_gate = jnp.sum(jnp.where(expert_ids == owner_index, gate_vals, 0.0), axis=1)
    gate_tile = jnp.broadcast_to(my_gate[None, :], (8, 128))
    pair = jnp.concatenate(
        [residual_in.reshape(2, HALF, OWN), jnp.broadcast_to(norm_gain, (2, 16, OWN))], axis=1
    )

    score_scale = (HD + ROPE) ** (-0.5)
    scores = (
        jnp.einsum("rhk,rlk->rhl", queries, cache, preferred_element_type=jnp.float32) * score_scale
    )
    places = lax.broadcasted_iota(jnp.int32, (1, 1, cache.shape[1]), 2)
    scores = jnp.where(places < lengths[:, None, None], scores, -jnp.inf)
    row_top = jnp.max(scores, axis=2, keepdims=True)
    exp_terms = jnp.exp(scores - row_top)
    attn_probs = (exp_terms / jnp.sum(exp_terms, axis=2, keepdims=True)).astype(jnp.bfloat16)
    latent_width = w_uv.shape[1]
    latent = jnp.einsum(
        "rhl,rlk->rhk", attn_probs, cache[:, :, :latent_width], preferred_element_type=jnp.float32
    ).astype(jnp.bfloat16)
    head_out = jnp.einsum("rhk,hkd->rhd", latent, w_uv, preferred_element_type=jnp.float32).astype(
        jnp.bfloat16
    )
    head_out = head_out.reshape(head_out.shape[0], -1)
    return layer_call(
        head_out,
        pair,
        gate_tile,
        w_out,
        w_gate.reshape(2, 8, OWN, 256),
        w_up.reshape(2, 8, OWN, 256),
        w_down[0],
    )


def solution(mesh):
    placed = (
        P(("side", "row"), "col", None),
        P(("side", "row"), None, None),
        P(("side", "row")),
        P("col", None, None),
        P("col", ("side", "row")),
        P("col", ("side", "row")),
        P(("side", "row")),
        P("col", None),
        P("col", None),
        P(("side", "row"), None, "col"),
        P(("side", "row"), None, "col"),
        P(("side", "row"), "col", None),
    )
    return jax.shard_map(
        shards, mesh=mesh, in_specs=placed, out_specs=P("col", ("side", "row")), check_vma=False
    )
```

time: 631 us -> 184 us (0.29)
  waiting for transfers between devices: 515 us -> 0 us
  Pallas kernels: 0 us -> 158 us
  blocking collectives: 43.3 us -> 0 us
  matrix products: 39.6 us -> 14.8 us
  between operations: 13.6 us -> 0.04 us
    all_gather x3 -> x0, waiting for transfers between devices: 259 us -> none  [the longest x1 154 us: shards(): row_piece = lax.all_gather(full_block, 'col', axis=0, tiled=True)]
    unnamed x8 -> x0, waiting for transfers between devices: 188 us -> none
    pallas_call x0 -> x1, Pallas kernels: none -> 158 us  [layer_call(): pl.pallas_call(layer_kernel, out_shape=jax.ShapeDtypeStruct((2 * HALF, OW...]
    reduce_scatter x1 -> x0, waiting for transfers between devices: 66.9 us -> none  [shards(): lax.psum_scatter(weighted.astype(jnp.bfloat16), ('side', 'row'), scatter_...]
    psum x1 -> x0, blocking collectives: 43.3 us -> none  [shards(): squares_total = lax.psum(jnp.sum(hidden * hidden, axis=1), ('side', 'row'))]
    dot_general x4 -> x0, matrix products: 24.7 us -> none  [the longest x1 8.49 us: shards(): gate_part = jnp.dot(row_piece, gate_dev, preferred_element_type=jnp.float32)]
  transfers between devices with their start and end apart: 6 -> 0, of which waited for: 6 -> 0; matrix products, arithmetic and copies ran while one was open for 0% -> 0% of each run, Pallas kernels for 0% -> 0%
where the time goes in v2:
time: 184 us
  Pallas kernels  158 us (86%)
  matrix products  14.8 us (8%)
  local copies, waits for them, and re-layouts  8.56 us (5%)
  other arithmetic  2.62 us (1%)
    pallas_call x1, Pallas kernels, layer_call(): pl.pallas_call(layer_kernel, out_shape=jax.ShapeDtypeStruct((2 * HALF, OW...  158 us
    dot_general x1, matrix products, shards(): jnp.einsum('rhl,rlk->rhk', attn_probs, cache[:, :, :latent_width], prefer...  6.73 us
    dot_general x1, matrix products, shards(): jnp.einsum('rhk,rlk->rhl', queries, cache, preferred_element_type=jnp.flo...  5.56 us
    unnamed x4, local copies, waits for them, and re-layouts  4.83 us

profile of v2, /device:TPU:1, one launch (start us, length us, event | category | flops | bytes accessed | tf_op | source)
XLA Modules:
  0.0 183.9 jit_solution(13776517512707944203)
XLA Ops:
  0.0 0.0 copy-start
  0.0 0.9 select_reduce_fusion
  0.9 0.6 broadcast_in_dim.32.gate_ref
  1.5 0.7 iota_compare_fusion
  2.2 0.7 broadcast_in_dim.30
  2.9 1.0 copy.14
  3.9 0.7 pad_maximum_fusion.pair_ref
  4.6 5.6 %fusion.4 = f32[64,16,128]{2,1,0:T(8,128)S(1)} fusion(bf16[64,16,576]{2,1,0:T(8,128)(2,1)} %param.12, bf16[64,128,576]{1,2,0:T(8,128)(2,1)} %param.13, pred[64,128]{1,0:T(8,128)(4,1)S(1)} %iota_compare_fusion), kind=kOutput, calls=%fused_computation.6 | convolution fusion | flops 151257088 | bytes 11149312 | tf_op jit(solution)/shard_map/rhk,rlk->rhl/dot_general | solution.py:603
  10.1 0.3 fusion.9
  10.5 6.7 %fusion.1 = bf16[64,16,512]{2,1,0:T(8,128)(2,1)} fusion(bf16[64,128,576]{1,2,0:T(8,128)(2,1)} %param.13, f32[64,16]{1,0:T(8,128)S(1)} %fusion.9, f32[64,16,128]{2,1,0:T(8,128)S(1)} %fusion.4), kind=kOutput, calls=%fused_computation.1 | convolution fusion | flops 134612096 | bytes 10518528 | tf_op jit(solution)/shard_map/rhl,rlk->rhk/dot_general | solution.py:611
  17.2 0.0 copy-done
  17.2 2.5 %fusion.6 = bf16[16,8,8,128]{3,2,1,0:T(8,128)(2,1)S(1)} fusion(bf16[16,512,128]{2,1,0:T(8,128)(2,1)S(1)} %copy-done, bf16[64,16,512]{2,1,0:T(8,128)(2,1)} %fusion.1), kind=kOutput, calls=%fused_computation.9 | convolution fusion | flops 134348800 | bytes 3407872 | tf_op jit(solution)/shard_map/rhk,hkd->rhd/dot_general | solution.py:614
  19.8 0.8 copy.22
  20.6 3.8 %copy.15.out_hbm = bf16[2048,448]{1,0:T(8,128)(2,1)} copy(bf16[2048,448]{0,1:T(8,128)(2,1)} %param.16) | data formatting | bytes 3670016 | tf_op args[4]
  24.4 157.9 %shard_map.118 = bf16[128,448]{1,0:T(8,128)(2,1)} custom-call(bf16[64,2048]{1,0:T(8,128)(2,1)} %bitcast.16, bf16[2,80,448]{2,1,0:T(8,128)(2,1)} %pad_maximum_fusion.pair_ref, f32[8,128]{1,0:T(8,128)} %broadcast_in_dim.32.gate_ref, bf16[2048,448]{1,0:T(8,128)(2,1)} %copy.15.out_hbm, bf16[2,8,448,256]{3,2,1,0:T(8,128)(2,1)} %bitcast.17, ...), custom_call_target="tpu_custom_call" | custom-call | flops 14680064000 | bytes 16777216 | tf_op jit(solution)/shard_map/pallas_call | solution.py:565
  182.3 1.7 copy.16
Async XLA Ops:
  0.0 17.2 %copy-start = (bf16[16,512,128]{2,1,0:T(8,128)(2,1)S(1)}, bf16[16,512,128]{2,1,0:T(8,128)(2,1)}, u32[]{:S(2)}) copy-start(bf16[16,512,128]{2,1,0:T(8,128)(2,1)} %param.15) | copy-start | bytes 6291460

commit v3 on v0

v3 whole, which is shorter than its diff:
```python
import jax
import jax.numpy as jnp
from jax import lax
from jax.experimental import pallas as pl
from jax.experimental.pallas import tpu as pltpu
from jax.sharding import PartitionSpec as P

D = 7168
ROPE = 64
HD = 128
HALF = 64
OWN = 448
PAIR = 896
MESH = pl.DeviceIdType.MESH
BF16 = jnp.bfloat16
F32 = jnp.float32

LANES = ((0, 384), (384, 256), (640, 256))
ORDERS = (
    (("x", "y", "z"), ("y", "z", "x"), ("z", "x", "y")),
    (("y", "z", "x"), ("z", "x", "y"), ("x", "y", "z")),
)
HEAD_LANES = ((0, 1152), (1152, 896))
SUM_LANES = ((0, 512), (512, 384))
LOW, HIGH, ALL = (0, 32), (32, 32), (0, 64)


class Place:
    def __init__(self):
        self.side, self.row, self.col = (lax.axis_index(name) for name in ("side", "row", "col"))
        z_hi, y = lax.div(self.row, 4), lax.rem(self.row, 4)
        z_lo, x = lax.div(self.col, 4), lax.rem(self.col, 4)
        at = {"x": x, "y": y, "z": z_hi * 2 + z_lo}
        self.coord = {a: [at[a]] + [lax.rem(at[a] + k, 4) for k in (1, 2, 3)] for a in "xyz"}
        self.bits = {a: [(lax.div(j, 2), lax.rem(j, 2)) for j in self.coord[a]] for a in "xyz"}
        self.sibling = (1 - self.side, self.row, self.col)
        self.ids = {"x": [], "y": [], "z": []}
        for k in range(4):
            high, low = self.bits["z"][k]
            self.ids["x"].append((self.side, self.row, z_lo * 4 + self.coord["x"][k]))
            self.ids["y"].append((self.side, z_hi * 4 + self.coord["y"][k], self.col))
            self.ids["z"].append((self.side, high * 4 + y, low * 4 + x))

    def view(self, ref, at, rows, lanes, lead=()):
        index = [slice(None)] * 6
        if "x" in at:
            index[1], index[2] = self.bits["x"][at["x"]]
        if "y" in at:
            index[4], index[5] = self.bits["y"][at["y"]]
        if "z" in at:
            index[3], index[0] = self.bits["z"][at["z"]]
        return ref.at[(*lead, *index, pl.ds(*rows), pl.ds(*lanes))]


def remote(src, dst, send_sem, recv_sem, device):
    return pltpu.make_async_remote_copy(
        src_ref=src,
        dst_ref=dst,
        send_sem=send_sem,
        recv_sem=recv_sem,
        device_id=device,
        device_id_type=MESH,
    )


class RingGather:
    def __init__(self, here, axis, bundle, halves, sems):
        self.here, self.axis, self.bundle, self.halves, self.sems = here, axis, bundle, halves, sems

    def copy(self, direction, piece):
        send, recv = self.sems
        up = (1, 3)[direction]
        half = self.halves[direction if piece != 1 else 1 - direction]
        ref = self.bundle(0 if piece < 2 else 4 - up, half)
        device = self.here.ids[self.axis][up]
        return remote(ref, ref, send.at[direction, piece], recv.at[direction, piece], device)

    def start(self):
        for piece in range(2):
            for direction in range(2):
                self.copy(direction, piece).start()

    def relay(self):
        for direction in range(2):
            self.copy(direction, 0).wait_recv()
            self.copy(direction, 2).start()

    def near(self):
        for direction in range(2):
            self.copy(direction, 1).wait_recv()

    def far(self):
        for direction in range(2):
            self.copy(direction, 2).wait_recv()

    def drain(self):
        for direction in range(2):
            for piece in range(3):
                self.copy(direction, piece).wait_send()


class RingScatter:
    def __init__(self, here, axis, bundle, halves, arrived, sems):
        self.here, self.axis, self.bundle, self.halves = here, axis, bundle, halves
        self.arrived, self.sems = arrived, sems

    def place(self, direction, piece):
        k = 2 if piece == 0 else (1, 3)[direction]
        return self.bundle(k, self.halves[direction if piece != 1 else 1 - direction])

    def copy(self, direction, piece):
        send, recv = self.sems
        return remote(
            self.place(direction, piece),
            self.arrived.at[direction, piece],
            send.at[direction, piece],
            recv.at[direction, piece],
            self.here.ids[self.axis][(1, 3)[direction]],
        )

    def start(self):
        for piece in range(2):
            for direction in range(2):
                self.copy(direction, piece).start()

    def relay(self):
        for direction in range(2):
            self.copy(direction, 0).wait_recv()
            target = self.place(direction, 2)
            target[...] = (target[...].astype(F32) + self.arrived[direction, 0].astype(F32)).astype(BF16)
            self.copy(direction, 2).start()

    def finish(self, use=None):
        for direction in range(2):
            self.copy(direction, 1).wait_recv()
            self.copy(direction, 2).wait_recv()
        for rows, (first, second) in zip(self.halves, ((2, 1), (1, 2))):
            target = self.bundle(0, rows)
            value = target[...].astype(F32) + (
                self.arrived[0, first].astype(F32) + self.arrived[1, second].astype(F32)
            )
            if use is None:
                target[...] = value.astype(BF16)
            else:
                use(rows, value)

    def drain(self):
        for direction in range(2):
            for piece in range(3):
                self.copy(direction, piece).wait_send()


def layer_kernel(
    head_ref, residual_ref, gain_ref, ids_ref, vals_ref, out_hbm, gate_hbm, up_hbm, down_hbm, out_ref,
    heads, proj, part_sums, z_early, z_late, x_early, x_late, pair, pair_sib, pair_all, hidden, square,
    rows_buf, weights, down, down_pairs, total, acts, squares, inverses, gates, columns,
    from_sibling, mixed, mixed_sib,
    load_sems, head_sems, flip_sems, sum_sems, pair_sems, proj_sems, small_send, small_recv,
    send_sems, recv_sems, share_send, share_recv, back_send, back_recv, *arrivals,
):
    here = Place()
    side, row, col, sibling = here.side, here.row, here.col, here.sibling
    (z_hi, z_lo), (x_hi, x_lo), (y_hi, y_lo) = (here.bits[axis][0] for axis in "zxy")
    x = here.coord["x"][0]
    far_z = here.ids["z"][2]
    flip_z = (side, row, lax.rem(col + 4, 8))

    def row_peer(k):
        return (side, lax.rem(row + k, 8), col)

    def col_peer(k):
        return (side, row, lax.rem(col + k, 8))


    loads = [
        pltpu.make_async_copy(
            source.at[core],
            weights.at[:, core, :, pl.ds(which * 256, 256)],
            load_sems.at[which * 2 + core],
        )
        for which, source in enumerate((gate_hbm, up_hbm))
        for core in range(2)
    ]
    load_proj = pltpu.make_async_copy(out_hbm, proj.at[side], load_sems.at[4])
    load_down = pltpu.make_async_copy(down_hbm, down, load_sems.at[5])
    heads[side, z_hi, y_hi, y_lo] = head_ref[...]

    barrier = pltpu.get_barrier_semaphore()
    peers = [sibling, *map(row_peer, range(1, 8)), *map(col_peer, range(1, 8)), here.ids["z"][1], here.ids["z"][3]]
    for peer in peers:
        pl.semaphore_signal(barrier, inc=1, device_id=peer, device_id_type=MESH)
    pl.semaphore_wait(barrier, len(peers))

    def head_view(which, at, rows):
        return heads.at[(side, *at, pl.ds(*rows), pl.ds(*HEAD_LANES[which]))]

    def head_ring(index, which, z):
        return RingGather(
            here,
            "y",
            lambda k, rows: head_view(which, (z, *here.bits["y"][k]), rows),
            (LOW, HIGH),
            (head_sems.at[0, index], head_sems.at[1, index]),
        )

    def head_flip(index, which, k):
        ref = head_view(which, (z_hi, *here.bits["y"][k]), ALL)
        return remote(ref, ref, flip_sems.at[0, index], flip_sems.at[1, index], far_z)

    flips = [head_flip(0, 0, 0)] + [head_flip(1 + k, 1, k) for k in range(4)]
    rings = [head_ring(0, 1, z_hi), head_ring(1, 0, z_hi), head_ring(2, 0, 1 - z_hi)]
    flips[0].start()
    rings[0].start()
    rings[1].start()
    flips[1].start()
    load_proj.start()
    for load in loads:
        load.start()
    load_down.start()

    owner = side * 8 + row
    chosen = jnp.where(ids_ref[...] == owner, vals_ref[...], 0.0)
    gates[col] = jnp.broadcast_to(jnp.sum(chosen, axis=0, keepdims=True), (8, 128))
    square[0:OWN] = residual_ref[...].astype(F32)
    square[OWN:512] = jnp.zeros((512 - OWN, 128), F32)
    residual = square[...].T.astype(BF16)
    for half in range(2):
        pair[half, 0:HALF] = residual[half * HALF : (half + 1) * HALF, 0:OWN]
        pair[half, HALF:80] = jnp.broadcast_to(gain_ref[...].astype(F32), (16, OWN)).astype(BF16)
    pair_copy = remote(pair.at[1 - side], pair_sib, pair_sems.at[0], pair_sems.at[1], sibling)
    pair_copy.start()
    proj_copy = remote(out_hbm, proj.at[side], proj_sems.at[0], proj_sems.at[1], sibling)
    proj_copy.start()
    def smalls(kind, ref, name):
        @pl.loop(0, 7)
        def _(k):
            peer = row_peer(k + 1) if kind == 1 else col_peer(k + 1)
            getattr(remote(ref, ref, small_send.at[kind, k], small_recv.at[kind, k], peer), name)()

    smalls(0, gates.at[col], "start")

    rings[0].relay()
    flips[0].wait_recv()
    rings[2].start()
    rings[0].near()
    flips[2].start()
    flips[4].start()
    rings[1].relay()
    rings[0].far()
    flips[3].start()

    pair_copy.wait_recv()

    @pl.when(side == 0)
    def _():
        pair_all[:, 0:OWN] = pair[0]
        pair_all[:, OWN:PAIR] = pair_sib[...]

    @pl.when(side == 1)
    def _():
        pair_all[:, 0:OWN] = pair_sib[...]
        pair_all[:, OWN:PAIR] = pair[1]

    rings[2].relay()
    for ring in rings[1:]:
        ring.near()
        ring.far()
    for flip in flips[1:]:
        flip.wait_recv()
    theirs = heads.at[side, :, :, 1 - side]
    head_share = remote(theirs, theirs, pair_sems.at[2], pair_sems.at[3], sibling)
    head_share.start()

    load_proj.wait()
    proj_copy.wait_recv()

    def project(source):
        lhs = heads[source, :, :, side].reshape(4 * HALF, 2048)
        value = lax.dot_general(
            lhs, proj[...].reshape(PAIR, 2048), (((1,), (1,)), ((), ())), preferred_element_type=F32
        )
        part_sums[source] = value.astype(BF16).reshape(4, HALF, PAIR)

    project(side)
    head_share.wait_recv()
    project(1 - side)

    def x_ring(which, lead, arrived):
        return RingScatter(
            here,
            "x",
            lambda k, rows: part_sums.at[lead, here.coord["x"][k], pl.ds(*rows), pl.ds(*SUM_LANES[which])],
            (LOW, HIGH),
            arrived,
            (sum_sems.at[0, which], sum_sems.at[1, which]),
        )

    early_flip = remote(
        part_sums.at[1 - z_lo, :, :, pl.ds(*SUM_LANES[1])], z_early, flip_sems.at[0, 5], flip_sems.at[1, 5], flip_z
    )
    early_flip.start()
    early_ring = x_ring(0, slice(None), x_early)
    early_ring.start()
    early_ring.relay()
    early_flip.wait_recv()
    mine = part_sums.at[z_lo, :, :, pl.ds(*SUM_LANES[1])]
    mine[...] = (mine[...].astype(F32) + z_early[...].astype(F32)).astype(BF16)
    late_ring = x_ring(1, z_lo, x_late)
    late_ring.start()
    early_ring.finish()
    late_flip = remote(
        part_sums.at[1 - z_lo, x, :, pl.ds(*SUM_LANES[0])], z_late, flip_sems.at[0, 6], flip_sems.at[1, 6], flip_z
    )
    late_flip.start()
    late_ring.relay()
    late_flip.wait_recv()
    left = pl.ds(*SUM_LANES[0])
    hidden[:, left] = pair_all[0:HALF, left].astype(F32) + (
        part_sums[z_lo, x, :, left].astype(F32) + z_late[...].astype(F32)
    )

    def right(rows, value):
        spot = (pl.ds(*rows), pl.ds(*SUM_LANES[1]))
        hidden[spot] = pair_all[spot].astype(F32) + value

    late_ring.finish(right)
    rows_buf[side, z_lo, x_hi, x_lo, z_hi, y_hi, y_lo] = (
        hidden[...] * pair_all[HALF : HALF + 1].astype(F32)
    ).astype(BF16)

    def per_core(step):
        for core in range(2):

            @pl.when(side == core)
            def _(core=core):
                step(ORDERS[core])

    def halves(t):
        return (t * 32, 16), (t * 32 + 16, 16)

    def gather_rings(t, phase, orders):
        for part in range(3):
            axis = orders[part][phase]
            own = {a: 0 for a in orders[part][phase:]}
            yield RingGather(
                here,
                axis,
                lambda k, rows, part=part, own=own, axis=axis: here.view(
                    rows_buf, {**own, axis: k}, rows, LANES[part], (side,)
                ),
                halves(t),
                (send_sems.at[0, t, part, phase], recv_sems.at[0, t, part, phase]),
            )

    def scatter_rings(t, phase, orders):
        for part in range(3):
            axis = orders[part][phase]
            done = {a: 0 for a in orders[part][:phase]}
            yield RingScatter(
                here,
                axis,
                lambda k, rows, part=part, done=done, axis=axis: here.view(
                    rows_buf, {**done, axis: k}, rows, LANES[part], (side,)
                ),
                halves(t),
                arrivals[part * 3 + phase].at[t],
                (send_sems.at[1, t, part, phase], recv_sems.at[1, t, part, phase]),
            )

    def each(rings, *names):
        def step(orders):
            made = list(rings(orders))
            for name in names:
                for ring in made:
                    getattr(ring, name)()

        per_core(step)

    def gather(t, phase, *names):
        each(lambda orders: gather_rings(t, phase, orders), *names)

    def scatter(t, phase, *names):
        each(lambda orders: scatter_rings(t, phase, orders), *names)

    def share(t, part, k, orders):
        ref = here.view(rows_buf, {orders[part][2]: k}, (t * 32, 32), LANES[part], (side,))
        return remote(ref, ref, share_send.at[t, part, k], share_recv.at[t, part, k], sibling)

    def shares(t, steps, name):
        def step(orders):
            for part in range(3):
                for k in steps:
                    getattr(share(t, part, k, orders), name)()

        per_core(step)

    def chunk(r):
        return lax.div(r, 4), lax.rem(lax.div(r, 2), 2), lax.rem(r, 2)

    def back(t, r):
        return remote(
            rows_buf.at[(1 - side,) + (slice(None),) * 3 + chunk(r) + (pl.ds(t * 32, 32),)],
            from_sibling.at[t, r],
            back_send.at[t, r],
            back_recv.at[t, r],
            sibling,
        )

    def experts(t):
        total[...] = jnp.zeros_like(total)

        @pl.loop(0, 8)
        def _(r):
            lhs = rows_buf[(slice(None),) * 4 + chunk(r) + (pl.ds(t * 32, 32),)].reshape(512, PAIR)
            total[...] += jnp.dot(lhs, weights[r].reshape(PAIR, 512), preferred_element_type=F32)

        for half in range(2):
            for c in range(8):
                first = half * 256 + c * 32
                scale = columns[t * 32 : t * 32 + 32, 8 + half * 8 + c : 9 + half * 8 + c]
                gate_col = columns[half * HALF + t * 32 : half * HALF + t * 32 + 32, c : c + 1]
                gate_part = total[first : first + 32, :256] * scale
                up_part = total[first : first + 32, 256:] * (scale * gate_col)
                acts[half, c * 32 : c * 32 + 32] = (
                    gate_part / (1.0 + jnp.exp(-gate_part)) * up_part
                ).astype(BF16)

    def down_theirs(t):
        @pl.loop(0, 8)
        def _(r):
            value = jnp.dot(acts[1 - side], down_pairs[r], preferred_element_type=F32).astype(BF16)
            rows_buf[(1 - side,) + (slice(None),) * 3 + chunk(r) + (pl.ds(t * 32, 32),)] = value.reshape(2, 2, 2, 32, PAIR)
            back(t, r).start()

    def down_own(t):
        @pl.loop(0, 8)
        def _(r):
            value = jnp.dot(acts[side], down_pairs[r], preferred_element_type=F32)
            back(t, r).wait_recv()
            value = value + from_sibling[t, r].reshape(256, PAIR).astype(F32)
            rows_buf[(side,) + (slice(None),) * 3 + chunk(r) + (pl.ds(t * 32, 32),)] = value.astype(BF16).reshape(
                2, 2, 2, 32, PAIR
            )

    def final(t):
        def step(orders):
            for part, ring in enumerate(scatter_rings(t, 2, orders)):

                def use(rows, value, part=part):
                    spot = (pl.ds(*rows), pl.ds(*LANES[part]))
                    mixed[spot] = (hidden[spot] + value).astype(BF16)

                ring.finish(use)

        per_core(step)

    gather(0, 0, "start")
    gather(1, 0, "start")
    value = hidden[...]
    columns[0:HALF] = jnp.broadcast_to(jnp.sum(value * value, axis=1, keepdims=True), (HALF, 128))
    columns[HALF:128] = jnp.zeros((HALF, 128), F32)
    squares[row] = columns[...].T[0:8]
    smalls(1, squares.at[row], "start")
    gather(0, 0, "relay")
    gather(1, 0, "relay")
    gather(0, 0, "near", "far")
    gather(0, 1, "start")
    gather(1, 0, "near", "far")
    gather(1, 1, "start")
    smalls(1, squares.at[row], "wait_recv")
    inverses[side, col] = lax.rsqrt(jnp.sum(squares[...], axis=0) / D + 1e-06)
    smalls(2, inverses.at[side, col], "start")
    gather(0, 1, "relay")
    gather(0, 1, "near")
    gather(1, 1, "relay")
    gather(0, 1, "far")
    gather(0, 2, "start")
    shares(0, (0,), "start")
    gather(1, 1, "near", "far")
    smalls(2, inverses.at[side, col], "wait_recv")
    inverse_share = remote(
        inverses.at[side], inverses.at[side], pair_sems.at[4], pair_sems.at[5], sibling
    )
    inverse_share.start()
    load_down.wait()
    for r in range(8):
        for core in range(2):
            down_pairs[r, :, core * OWN : (core + 1) * OWN] = down[
                :, (core * 8 + r) * OWN : (core * 8 + r + 1) * OWN
            ]
    gather(0, 2, "relay")
    gather(1, 2, "start")
    shares(1, (0,), "start")
    gather(0, 2, "near")
    shares(0, (1, 3), "start")
    smalls(0, gates.at[col], "wait_recv")
    inverse_share.wait_recv()
    columns[...] = jnp.zeros_like(columns)
    for c in range(8):
        columns[c : c + 1] = gates[c, 0:1]
        columns[8 + c : 9 + c] = inverses[0, c, 0:1]
        columns[16 + c : 17 + c] = inverses[1, c, 0:1]
    columns[...] = columns[...].T
    for load in loads:
        load.wait()
    gather(0, 2, "far")
    shares(0, (2,), "start")
    shares(0, (0, 1, 2, 3), "wait_recv")
    experts(0)
    gather(1, 2, "relay")
    down_theirs(0)
    gather(1, 2, "near")
    shares(1, (1, 3), "start")
    for phase in range(3):
        gather(0, phase, "drain")
    shares(0, (0, 1, 2, 3), "wait_send")
    down_own(0)
    gather(1, 2, "far")
    shares(1, (2,), "start")
    scatter(0, 0, "start")
    shares(1, (0, 1, 2, 3), "wait_recv")
    experts(1)
    scatter(0, 0, "relay")
    down_theirs(1)
    for phase in range(3):
        gather(1, phase, "drain")
    shares(1, (0, 1, 2, 3), "wait_send")
    down_own(1)
    scatter(1, 0, "start")
    scatter(0, 0, "finish")
    scatter(0, 1, "start")
    scatter(1, 0, "relay")
    scatter(0, 1, "relay")
    scatter(0, 1, "finish")
    scatter(0, 2, "start")
    scatter(0, 2, "relay")
    scatter(1, 0, "finish")
    scatter(1, 1, "start")
    final(0)
    scatter(1, 1, "relay", "finish")
    scatter(1, 2, "start", "relay")
    final(1)

    last = remote(mixed, mixed_sib, pair_sems.at[6], pair_sems.at[7], sibling)
    last.start()
    last.wait_recv()

    def transposed(top, bottom):
        square[0:PAIR // 2, 0:HALF] = top.astype(F32).T
        square[0:PAIR // 2, HALF:128] = bottom.astype(F32).T
        out_ref[...] = square[0:OWN].astype(BF16)

    @pl.when(side == 0)
    def _():
        transposed(mixed[:, 0:OWN], mixed_sib[:, 0:OWN])

    @pl.when(side == 1)
    def _():
        transposed(mixed_sib[:, OWN:PAIR], mixed[:, OWN:PAIR])

    last.wait_send()
    for ring in (*rings, early_ring, late_ring):
        ring.drain()
    for copy in (
        *flips, early_flip, late_flip, pair_copy, proj_copy, head_share, inverse_share,
    ):
        copy.wait_send()
    smalls(0, gates.at[col], "wait_send")
    smalls(1, squares.at[row], "wait_send")
    smalls(2, inverses.at[side, col], "wait_send")
    for t in range(2):
        for phase in range(3):
            scatter(t, phase, "drain")

        @pl.loop(0, 8)
        def _(r, t=t):
            back(t, r).wait_send()


ARRIVALS = [
    (2, 2, 3, *(2,) * (4 - 2 * phase), 16, LANES[part][1]) for part in range(3) for phase in range(3)
]

VMEM = pl.BlockSpec(memory_space=pltpu.VMEM)
ANY = pl.BlockSpec(memory_space=pl.ANY)
DMA = pltpu.SemaphoreType.DMA


def layer_call(*args):
    scratch = [
        pltpu.VMEM((2, 2, 2, 2, HALF, 2048), BF16),
        pltpu.VMEM((2, OWN, 2048), BF16),
        pltpu.VMEM((2, 4, HALF, PAIR), BF16),
        pltpu.VMEM((4, HALF, SUM_LANES[1][1]), BF16),
        pltpu.VMEM((HALF, SUM_LANES[0][1]), BF16),
        pltpu.VMEM((2, 3, 2, 32, SUM_LANES[0][1]), BF16),
        pltpu.VMEM((2, 3, 32, SUM_LANES[1][1]), BF16),
        pltpu.VMEM((2, 80, OWN), BF16),
        pltpu.VMEM((80, OWN), BF16),
        pltpu.VMEM((80, PAIR), BF16),
        pltpu.VMEM((HALF, PAIR), F32),
        pltpu.VMEM((512, 128), F32),
        pltpu.VMEM((2, 2, 2, 2, 2, 2, 2, HALF, PAIR), BF16),
        pltpu.VMEM((8, 2, OWN, 512), BF16),
        pltpu.VMEM((256, D), BF16),
        pltpu.VMEM((8, 256, PAIR), BF16),
        pltpu.VMEM((512, 512), F32),
        pltpu.VMEM((2, 256, 256), BF16),
        pltpu.VMEM((8, 8, 128), F32),
        pltpu.VMEM((2, 8, 8, 128), F32),
        pltpu.VMEM((8, 8, 128), F32),
        pltpu.VMEM((128, 128), F32),
        pltpu.VMEM((2, 8, 2, 2, 2, 32, PAIR), BF16),
        pltpu.VMEM((HALF, PAIR), BF16),
        pltpu.VMEM((HALF, PAIR), BF16),
        DMA((6,)),
        DMA((2, 3, 2, 3)),
        DMA((2, 7)),
        DMA((2, 2, 2, 3)),
        DMA((8,)),
        DMA((2,)),
        DMA((3, 7)),
        DMA((3, 7)),
        DMA((2, 2, 3, 3, 2, 3)),
        DMA((2, 2, 3, 3, 2, 3)),
        DMA((2, 3, 4)),
        DMA((2, 3, 4)),
        DMA((2, 8)),
        DMA((2, 8)),
        *[pltpu.VMEM(shape, BF16) for shape in ARRIVALS],
    ]
    return pl.pallas_call(
        layer_kernel,
        out_shape=jax.ShapeDtypeStruct((OWN, 2 * HALF), BF16),
        in_specs=[VMEM] * 5 + [ANY] * 4,
        out_specs=VMEM,
        scratch_shapes=scratch,
        compiler_params=pltpu.CompilerParams(
            collective_id=0, has_side_effects=True, vmem_limit_bytes=58 * 2**20
        ),
        cost_estimate=pl.CostEstimate(
            flops=2 * 1024 * 7168 * 1000, bytes_accessed=16 * 2**20, transcendentals=2**18
        ),
    )(*args)


def shards(
    queries,
    cache,
    lengths,
    w_uv,
    w_out,
    residual_in,
    norm_gain,
    expert_ids,
    gate_vals,
    w_gate,
    w_up,
    w_down,
):
    score_scale = (HD + ROPE) ** (-0.5)
    scores = (
        jnp.einsum("rhk,rlk->rhl", queries, cache, preferred_element_type=jnp.float32) * score_scale
    )
    places = lax.broadcasted_iota(jnp.int32, (1, 1, cache.shape[1]), 2)
    scores = jnp.where(places < lengths[:, None, None], scores, -jnp.inf)
    row_top = jnp.max(scores, axis=2, keepdims=True)
    exp_terms = jnp.exp(scores - row_top)
    attn_probs = (exp_terms / jnp.sum(exp_terms, axis=2, keepdims=True)).astype(jnp.bfloat16)
    latent_width = w_uv.shape[1]
    latent = jnp.einsum(
        "rhl,rlk->rhk", attn_probs, cache[:, :, :latent_width], preferred_element_type=jnp.float32
    ).astype(jnp.bfloat16)
    head_out = jnp.einsum("rhk,hkd->rhd", latent, w_uv, preferred_element_type=jnp.float32).astype(
        jnp.bfloat16
    )
    head_out = head_out.reshape(head_out.shape[0], -1)
    return layer_call(
        head_out,
        residual_in.T,
        norm_gain.reshape(1, OWN),
        expert_ids.T,
        gate_vals.T,
        w_out.T,
        w_gate.reshape(2, 8, OWN, 256),
        w_up.reshape(2, 8, OWN, 256),
        w_down[0],
    ).T


def solution(mesh):
    placed = (
        P(("side", "row"), "col", None),
        P(("side", "row"), None, None),
        P(("side", "row")),
        P("col", None, None),
        P("col", ("side", "row")),
        P("col", ("side", "row")),
        P(("side", "row")),
        P("col", None),
        P("col", None),
        P(("side", "row"), None, "col"),
        P(("side", "row"), None, "col"),
        P(("side", "row"), "col", None),
    )
    return jax.shard_map(
        shards, mesh=mesh, in_specs=placed, out_specs=P("col", ("side", "row")), check_vma=False
    )
```

time: 631 us -> 162 us (0.26)
  waiting for transfers between devices: 515 us -> 0 us
  Pallas kernels: 0 us -> 143 us
  blocking collectives: 43.3 us -> 0 us
  matrix products: 39.6 us -> 14.9 us
  between operations: 13.6 us -> 0.03 us
  local copies, waits for them, and re-layouts: 10.7 us -> 2.89 us
    all_gather x3 -> x0, waiting for transfers between devices: 259 us -> none  [the longest x1 154 us: shards(): row_piece = lax.all_gather(full_block, 'col', axis=0, tiled=True)]
    unnamed x8 -> x0, waiting for transfers between devices: 188 us -> none
    pallas_call x0 -> x1, Pallas kernels: none -> 143 us  [layer_call(): pl.pallas_call(layer_kernel, out_shape=jax.ShapeDtypeStruct((OWN, 2 * HAL...]
    reduce_scatter x1 -> x0, waiting for transfers between devices: 66.9 us -> none  [shards(): lax.psum_scatter(weighted.astype(jnp.bfloat16), ('side', 'row'), scatter_...]
    psum x1 -> x0, blocking collectives: 43.3 us -> none  [shards(): squares_total = lax.psum(jnp.sum(hidden * hidden, axis=1), ('side', 'row'))]
    dot_general x4 -> x0, matrix products: 24.7 us -> none  [the longest x1 8.49 us: shards(): gate_part = jnp.dot(row_piece, gate_dev, preferred_element_type=jnp.float32)]
    unnamed x21 -> x5, local copies, waits for them, and re-layouts: 9.99 us -> 1.56 us
  transfers between devices with their start and end apart: 6 -> 0, of which waited for: 6 -> 0; matrix products, arithmetic and copies ran while one was open for 0% -> 0% of each run, Pallas kernels for 0% -> 0%
where the time goes in v3:
time: 162 us
  Pallas kernels  143 us (88%)
  matrix products  14.9 us (9%)
  local copies, waits for them, and re-layouts  2.89 us (2%)
    pallas_call x1, Pallas kernels, layer_call(): pl.pallas_call(layer_kernel, out_shape=jax.ShapeDtypeStruct((OWN, 2 * HAL...  143 us
    dot_general x1, matrix products, shards(): jnp.einsum('rhl,rlk->rhk', attn_probs, cache[:, :, :latent_width], prefer...  6.73 us
    dot_general x1, matrix products, shards(): jnp.einsum('rhk,rlk->rhl', queries, cache, preferred_element_type=jnp.flo...  5.57 us

profile of v3, /device:TPU:1, one launch (start us, length us, event | category | flops | bytes accessed | tf_op | source)
XLA Modules:
  0.0 162.1 jit_solution(16497344050929076972)
XLA Ops:
  0.0 0.0 copy-start
  0.0 0.9 iota_compare_fusion
  0.9 5.6 %fusion.4 = f32[64,16,128]{2,1,0:T(8,128)S(1)} fusion(bf16[64,16,576]{2,1,0:T(8,128)(2,1)} %param.12, bf16[64,128,576]{1,2,0:T(8,128)(2,1)} %param.13, pred[64,128]{1,0:T(8,128)(4,1)S(1)} %iota_compare_fusion), kind=kOutput, calls=%fused_computation.6 | convolution fusion | flops 151257088 | bytes 11149312 | tf_op jit(solution)/shard_map/rhk,rlk->rhl/dot_general | solution.py:663
  6.5 0.3 fusion.9
  6.8 6.7 %fusion.1 = bf16[64,16,512]{2,1,0:T(8,128)(2,1)} fusion(bf16[64,128,576]{1,2,0:T(8,128)(2,1)} %param.13, f32[64,16]{1,0:T(8,128)S(1)} %fusion.9, f32[64,16,128]{2,1,0:T(8,128)S(1)} %fusion.4), kind=kOutput, calls=%fused_computation.1 | convolution fusion | flops 134612096 | bytes 10518528 | tf_op jit(solution)/shard_map/rhl,rlk->rhk/dot_general | solution.py:671
  13.6 0.0 copy-done
  13.6 0.0 copy-start.1
  13.6 2.6 %fusion.6 = bf16[16,8,8,128]{3,2,1,0:T(8,128)(2,1)S(1)} fusion(bf16[16,512,128]{2,1,0:T(8,128)(2,1)S(1)} %copy-done, bf16[64,16,512]{2,1,0:T(8,128)(2,1)} %fusion.1), kind=kOutput, calls=%fused_computation.9 | convolution fusion | flops 134348800 | bytes 3407872 | tf_op jit(solution)/shard_map/rhk,hkd->rhd/dot_general | solution.py:674
  16.1 0.7 copy.19
  16.9 0.0 copy-done.1
  16.9 0.6 reshape.36.gain_ref
  17.4 143.1 %shard_map.118 = bf16[448,128]{1,0:T(8,128)(2,1)} custom-call(bf16[64,2048]{1,0:T(8,128)(2,1)} %bitcast.19, bf16[448,128]{1,0:T(8,128)(2,1)} %bitcast.25, bf16[1,448]{1,0:T(2,128)(2,1)} %reshape.36.gain_ref, s32[8,128]{1,0:T(8,128)} %bitcast.26, f32[8,128]{1,0:T(8,128)} %bitcast.27, bf16[448,2048]{1,0:T(8,128)(2,1)} %bitcast.24, ...), custom_call_target="tpu_custom_call" | custom-call | flops 14680064000 | bytes 16777216 | tf_op jit(solution)/shard_map/pallas_call | solution.py:632
  160.6 1.6 copy.21
Async XLA Ops:
  0.0 13.6 %copy-start = (bf16[16,512,128]{2,1,0:T(8,128)(2,1)S(1)}, bf16[16,512,128]{2,1,0:T(8,128)(2,1)}, u32[]{:S(2)}) copy-start(bf16[16,512,128]{2,1,0:T(8,128)(2,1)} %param.15) | copy-start | bytes 6291460
  13.6 3.3 %copy-start.1 = (bf16[448]{0:T(512)(128)(2,1)S(1)}, bf16[448]{0:T(512)(128)(2,1)}, u32[]{:S(2)}) copy-start(bf16[448]{0:T(512)(128)(2,1)} %param.18) | copy-start | bytes 2692

commit v4 on v3

--- a/solution.py
+++ b/solution.py
@@ -23,6 +23,9 @@
 HEAD_LANES = ((0, 1152), (1152, 896))
 SUM_LANES = ((0, 512), (512, 384))
 LOW, HIGH, ALL = (0, 32), (32, 32), (0, 64)
+DIRECT_GATHERS = ((0, 0), (1, 0), (0, 1))
+DIRECT_SCATTERS = ((0, 2), (1, 1), (1, 2))
+GROUP = 8
 
 
 class Place:
@@ -150,13 +153,74 @@
                 self.copy(direction, piece).wait_send()
 
 
+class DirectGather:
+    def __init__(self, here, axis, bundle, halves, sems):
+        self.here, self.axis, self.bundle, self.sems = here, axis, bundle, sems
+        self.rows = (halves[0][0], 2 * halves[0][1])
+
+    def copies(self):
+        send, recv = self.sems
+        ref = self.bundle(0, self.rows)
+        for k in (2, 1, 3):
+            yield remote(ref, ref, send.at[0, k - 1], recv.at[0, k - 1], self.here.ids[self.axis][k])
+
+    def start(self):
+        for copy in self.copies():
+            copy.start()
+
+    def far(self):
+        for copy in self.copies():
+            copy.wait_recv()
+
+    def drain(self):
+        for copy in self.copies():
+            copy.wait_send()
+
+
+class DirectScatter:
+    def __init__(self, here, axis, bundle, halves, arrived, sems):
+        self.here, self.axis, self.bundle, self.arrived, self.sems = here, axis, bundle, arrived, sems
+        self.rows = (halves[0][0], 2 * halves[0][1])
+
+    def copies(self):
+        send, recv = self.sems
+        for k in (2, 1, 3):
+            yield remote(
+                self.bundle(k, self.rows),
+                self.arrived.at[k - 1],
+                send.at[0, k - 1],
+                recv.at[0, k - 1],
+                self.here.ids[self.axis][k],
+            )
+
+    def start(self):
+        for copy in self.copies():
+            copy.start()
+
+    def finish(self, use=None):
+        for copy in self.copies():
+            copy.wait_recv()
+        target = self.bundle(0, self.rows)
+        value = target[...].astype(F32) + (
+            self.arrived[0].astype(F32) + (self.arrived[1].astype(F32) + self.arrived[2].astype(F32))
+        )
+        if use is None:
+            target[...] = value.astype(BF16)
+        else:
+            use(self.rows, value)
+
+    def drain(self):
+        for copy in self.copies():
+            copy.wait_send()
+
+
 def layer_kernel(
     head_ref, residual_ref, gain_ref, ids_ref, vals_ref, out_hbm, gate_hbm, up_hbm, down_hbm, out_ref,
     heads, proj, part_sums, z_early, z_late, x_early, x_late, pair, pair_sib, pair_all, hidden, square,
     rows_buf, weights, down, down_pairs, total, acts, squares, inverses, gates, columns,
     from_sibling, mixed, mixed_sib,
     load_sems, head_sems, flip_sems, sum_sems, pair_sems, proj_sems, small_send, small_recv,
-    send_sems, recv_sems, share_send, share_recv, back_send, back_recv, *arrivals,
+    send_sems, recv_sems, share_send, share_recv, back_send, back_recv, last_sems, *arrivals,
 ):
     here = Place()
     side, row, col, sibling = here.side, here.row, here.col, here.sibling
@@ -285,8 +349,8 @@
     head_share.wait_recv()
     project(1 - side)
 
-    def x_ring(which, lead, arrived):
-        return RingScatter(
+    def x_ring(kind, which, lead, arrived):
+        return kind(
             here,
             "x",
             lambda k, rows: part_sums.at[lead, here.coord["x"][k], pl.ds(*rows), pl.ds(*SUM_LANES[which])],
@@ -299,20 +363,19 @@
         part_sums.at[1 - z_lo, :, :, pl.ds(*SUM_LANES[1])], z_early, flip_sems.at[0, 5], flip_sems.at[1, 5], flip_z
     )
     early_flip.start()
-    early_ring = x_ring(0, slice(None), x_early)
+    early_ring = x_ring(RingScatter, 0, slice(None), x_early)
     early_ring.start()
     early_ring.relay()
     early_flip.wait_recv()
     mine = part_sums.at[z_lo, :, :, pl.ds(*SUM_LANES[1])]
     mine[...] = (mine[...].astype(F32) + z_early[...].astype(F32)).astype(BF16)
-    late_ring = x_ring(1, z_lo, x_late)
+    late_ring = x_ring(DirectScatter, 1, z_lo, x_late)
     late_ring.start()
     early_ring.finish()
     late_flip = remote(
         part_sums.at[1 - z_lo, x, :, pl.ds(*SUM_LANES[0])], z_late, flip_sems.at[0, 6], flip_sems.at[1, 6], flip_z
     )
     late_flip.start()
-    late_ring.relay()
     late_flip.wait_recv()
     left = pl.ds(*SUM_LANES[0])
     hidden[:, left] = pair_all[0:HALF, left].astype(F32) + (
@@ -342,7 +405,7 @@
         for part in range(3):
             axis = orders[part][phase]
             own = {a: 0 for a in orders[part][phase:]}
-            yield RingGather(
+            yield (DirectGather if (t, phase) in DIRECT_GATHERS else RingGather)(
                 here,
                 axis,
                 lambda k, rows, part=part, own=own, axis=axis: here.view(
@@ -356,14 +419,14 @@
         for part in range(3):
             axis = orders[part][phase]
             done = {a: 0 for a in orders[part][:phase]}
-            yield RingScatter(
+            yield (DirectScatter if (t, phase) in DIRECT_SCATTERS else RingScatter)(
                 here,
                 axis,
                 lambda k, rows, part=part, done=done, axis=axis: here.view(
                     rows_buf, {**done, axis: k}, rows, LANES[part], (side,)
                 ),
                 halves(t),
-                arrivals[part * 3 + phase].at[t],
+                arrivals[(t * 3 + phase) * 3 + part],
                 (send_sems.at[1, t, part, phase], recv_sems.at[1, t, part, phase]),
             )
 
@@ -406,24 +469,21 @@
             sibling,
         )
 
-    def experts(t):
+    def experts(t, half, place):
         total[...] = jnp.zeros_like(total)
 
         @pl.loop(0, 8)
         def _(r):
-            lhs = rows_buf[(slice(None),) * 4 + chunk(r) + (pl.ds(t * 32, 32),)].reshape(512, PAIR)
+            lhs = rows_buf[(half,) + (slice(None),) * 3 + chunk(r) + (pl.ds(t * 32, 32),)].reshape(256, PAIR)
             total[...] += jnp.dot(lhs, weights[r].reshape(PAIR, 512), preferred_element_type=F32)
 
-        for half in range(2):
-            for c in range(8):
-                first = half * 256 + c * 32
-                scale = columns[t * 32 : t * 32 + 32, 8 + half * 8 + c : 9 + half * 8 + c]
-                gate_col = columns[half * HALF + t * 32 : half * HALF + t * 32 + 32, c : c + 1]
-                gate_part = total[first : first + 32, :256] * scale
-                up_part = total[first : first + 32, 256:] * (scale * gate_col)
-                acts[half, c * 32 : c * 32 + 32] = (
-                    gate_part / (1.0 + jnp.exp(-gate_part)) * up_part
-                ).astype(BF16)
+        gate_rows = columns[pl.ds(pl.multiple_of(half * HALF + t * 32, 32), 32)]
+        for c in range(8):
+            first = c * 32
+            scale = columns[t * 32 : t * 32 + 32, place + c : place + c + 1]
+            gate_part = total[first : first + 32, :256] * scale
+            up_part = total[first : first + 32, 256:] * (scale * gate_rows[:, c : c + 1])
+            acts[half, first : first + 32] = (gate_part / (1.0 + jnp.exp(-gate_part)) * up_part).astype(BF16)
 
     def down_theirs(t):
         @pl.loop(0, 8)
@@ -454,6 +514,16 @@
 
         per_core(step)
 
+    def experts_own(t):
+        experts(t, side, 8)
+
+    def experts_theirs(t):
+        experts(t, 1 - side, 16)
+
+    def last(t):
+        rows = pl.ds(t * 32, 32)
+        return remote(mixed.at[rows], mixed_sib.at[rows], last_sems.at[0, t], last_sems.at[1, t], sibling)
+
     gather(0, 0, "start")
     gather(1, 0, "start")
     value = hidden[...]
@@ -461,21 +531,17 @@
     columns[HALF:128] = jnp.zeros((HALF, 128), F32)
     squares[row] = columns[...].T[0:8]
     smalls(1, squares.at[row], "start")
-    gather(0, 0, "relay")
-    gather(1, 0, "relay")
-    gather(0, 0, "near", "far")
+    gather(0, 0, "far")
     gather(0, 1, "start")
-    gather(1, 0, "near", "far")
+    gather(1, 0, "far")
     gather(1, 1, "start")
     smalls(1, squares.at[row], "wait_recv")
     inverses[side, col] = lax.rsqrt(jnp.sum(squares[...], axis=0) / D + 1e-06)
     smalls(2, inverses.at[side, col], "start")
-    gather(0, 1, "relay")
-    gather(0, 1, "near")
-    gather(1, 1, "relay")
     gather(0, 1, "far")
     gather(0, 2, "start")
     shares(0, (0,), "start")
+    gather(1, 1, "relay")
     gather(1, 1, "near", "far")
     smalls(2, inverses.at[side, col], "wait_recv")
     inverse_share = remote(
@@ -498,16 +564,17 @@
     columns[...] = jnp.zeros_like(columns)
     for c in range(8):
         columns[c : c + 1] = gates[c, 0:1]
-        columns[8 + c : 9 + c] = inverses[0, c, 0:1]
-        columns[16 + c : 17 + c] = inverses[1, c, 0:1]
+        columns[8 + c : 9 + c] = inverses[side, c, 0:1]
+        columns[16 + c : 17 + c] = inverses[1 - side, c, 0:1]
     columns[...] = columns[...].T
     for load in loads:
         load.wait()
     gather(0, 2, "far")
     shares(0, (2,), "start")
+    gather(1, 2, "relay")
+    experts_own(0)
     shares(0, (0, 1, 2, 3), "wait_recv")
-    experts(0)
-    gather(1, 2, "relay")
+    experts_theirs(0)
     down_theirs(0)
     gather(1, 2, "near")
     shares(1, (1, 3), "start")
@@ -515,13 +582,14 @@
         gather(0, phase, "drain")
     shares(0, (0, 1, 2, 3), "wait_send")
     down_own(0)
+    scatter(0, 0, "start")
     gather(1, 2, "far")
     shares(1, (2,), "start")
-    scatter(0, 0, "start")
+    experts_own(1)
     shares(1, (0, 1, 2, 3), "wait_recv")
-    experts(1)
+    experts_theirs(1)
+    down_theirs(1)
     scatter(0, 0, "relay")
-    down_theirs(1)
     for phase in range(3):
         gather(1, phase, "drain")
     shares(1, (0, 1, 2, 3), "wait_send")
@@ -533,17 +601,16 @@
     scatter(0, 1, "relay")
     scatter(0, 1, "finish")
     scatter(0, 2, "start")
-    scatter(0, 2, "relay")
+    final(0)
+    last(0).start()
     scatter(1, 0, "finish")
     scatter(1, 1, "start")
-    final(0)
-    scatter(1, 1, "relay", "finish")
-    scatter(1, 2, "start", "relay")
+    scatter(1, 1, "finish")
+    scatter(1, 2, "start")
     final(1)
-
-    last = remote(mixed, mixed_sib, pair_sems.at[6], pair_sems.at[7], sibling)
-    last.start()
-    last.wait_recv()
+    last(1).start()
+    for t in range(2):
+        last(t).wait_recv()
 
     def transposed(top, bottom):
         square[0:PAIR // 2, 0:HALF] = top.astype(F32).T
@@ -558,7 +625,8 @@
     def _():
         transposed(mixed_sib[:, OWN:PAIR], mixed[:, OWN:PAIR])
 
-    last.wait_send()
+    for t in range(2):
+        last(t).wait_send()
     for ring in (*rings, early_ring, late_ring):
         ring.drain()
     for copy in (
@@ -578,12 +646,71 @@
 
 
 ARRIVALS = [
-    (2, 2, 3, *(2,) * (4 - 2 * phase), 16, LANES[part][1]) for part in range(3) for phase in range(3)
+    (
+        *((3,) if (t, phase) in DIRECT_SCATTERS else (2, 3)),
+        *(2,) * (4 - 2 * phase),
+        32 if (t, phase) in DIRECT_SCATTERS else 16,
+        LANES[part][1],
+    )
+    for t in range(2)
+    for phase in range(3)
+    for part in range(3)
 ]
 
 VMEM = pl.BlockSpec(memory_space=pltpu.VMEM)
 ANY = pl.BlockSpec(memory_space=pl.ANY)
 DMA = pltpu.SemaphoreType.DMA
+
+
+def attend_kernel(lengths_ref, queries_ref, cache_ref, up_ref, out_ref, latent):
+    step = pl.program_id(0)
+    lane = lax.broadcasted_iota(jnp.int32, (16, 128), 1)
+    scores = []
+    for i in range(GROUP):
+        score = jnp.dot(queries_ref[i], cache_ref[i], preferred_element_type=F32) * (HD + ROPE) ** (-0.5)
+        scores.append(jnp.where(lane < lengths_ref[step * GROUP + i], score, -jnp.inf))
+    scores = jnp.concatenate(scores, axis=0)
+    terms = jnp.exp(scores - jnp.max(scores, axis=1, keepdims=True))
+    probs = (terms / jnp.sum(terms, axis=1, keepdims=True)).astype(BF16)
+    for i in range(GROUP):
+        value = lax.dot_general(
+            probs[i * 16 : (i + 1) * 16],
+            cache_ref[i, 0:512],
+            (((1,), (1,)), ((), ())),
+            preferred_element_type=F32,
+        )
+        for k in range(4):
+            latent[k, pl.ds(pl.multiple_of((step * GROUP + i) * 16, 16), 16)] = value[:, k * 128 : k * 128 + 128]
+
+    @pl.when(step == HALF // GROUP - 1)
+    def _():
+        for head in range(16):
+            rows = jnp.concatenate(
+                [latent[k, pl.ds(head, HALF, stride=16)] for k in range(4)], axis=1
+            ).astype(BF16)
+            out_ref[:, head * HD : (head + 1) * HD] = jnp.dot(
+                rows, up_ref[head], preferred_element_type=F32
+            ).astype(BF16)
+
+
+def attend_call(lengths, queries, cache, w_uv):
+    return pl.pallas_call(
+        attend_kernel,
+        out_shape=jax.ShapeDtypeStruct((HALF, 16 * HD), BF16),
+        grid=(HALF // GROUP,),
+        in_specs=[
+            pl.BlockSpec(memory_space=pltpu.SMEM),
+            pl.BlockSpec((GROUP, 16, 576), lambda i: (i, 0, 0)),
+            pl.BlockSpec((GROUP, 576, 128), lambda i: (i, 0, 0)),
+            pl.BlockSpec((16, 512, HD), lambda i: (0, 0, 0)),
+        ],
+        out_specs=pl.BlockSpec((HALF, 16 * HD), lambda i: (0, 0)),
+        scratch_shapes=[pltpu.VMEM((4, HALF * 16, 128), F32)],
+        compiler_params=pltpu.CompilerParams(vmem_limit_bytes=58 * 2**20),
+        cost_estimate=pl.CostEstimate(
+            flops=2 * 64 * 16 * 128 * 1700, bytes_accessed=14 * 2**20, transcendentals=2**17
+        ),
+    )(lengths, queries, cache, w_uv)
 
 
 def layer_call(*args):
@@ -594,7 +721,7 @@
         pltpu.VMEM((4, HALF, SUM_LANES[1][1]), BF16),
         pltpu.VMEM((HALF, SUM_LANES[0][1]), BF16),
         pltpu.VMEM((2, 3, 2, 32, SUM_LANES[0][1]), BF16),
-        pltpu.VMEM((2, 3, 32, SUM_LANES[1][1]), BF16),
+        pltpu.VMEM((3, HALF, SUM_LANES[1][1]), BF16),
         pltpu.VMEM((2, 80, OWN), BF16),
         pltpu.VMEM((80, OWN), BF16),
         pltpu.VMEM((80, PAIR), BF16),
@@ -604,7 +731,7 @@
         pltpu.VMEM((8, 2, OWN, 512), BF16),
         pltpu.VMEM((256, D), BF16),
         pltpu.VMEM((8, 256, PAIR), BF16),
-        pltpu.VMEM((512, 512), F32),
+        pltpu.VMEM((256, 512), F32),
         pltpu.VMEM((2, 256, 256), BF16),
         pltpu.VMEM((8, 8, 128), F32),
         pltpu.VMEM((2, 8, 8, 128), F32),
@@ -627,6 +754,7 @@
         DMA((2, 3, 4)),
         DMA((2, 8)),
         DMA((2, 8)),
+        DMA((2, 2)),
         *[pltpu.VMEM(shape, BF16) for shape in ARRIVALS],
     ]
     return pl.pallas_call(
@@ -658,23 +786,7 @@
     w_up,
     w_down,
 ):
-    score_scale = (HD + ROPE) ** (-0.5)
-    scores = (
-        jnp.einsum("rhk,rlk->rhl", queries, cache, preferred_element_type=jnp.float32) * score_scale
-    )
-    places = lax.broadcasted_iota(jnp.int32, (1, 1, cache.shape[1]), 2)
-    scores = jnp.where(places < lengths[:, None, None], scores, -jnp.inf)
-    row_top = jnp.max(scores, axis=2, keepdims=True)
-    exp_terms = jnp.exp(scores - row_top)
-    attn_probs = (exp_terms / jnp.sum(exp_terms, axis=2, keepdims=True)).astype(jnp.bfloat16)
-    latent_width = w_uv.shape[1]
-    latent = jnp.einsum(
-        "rhl,rlk->rhk", attn_probs, cache[:, :, :latent_width], preferred_element_type=jnp.float32
-    ).astype(jnp.bfloat16)
-    head_out = jnp.einsum("rhk,hkd->rhd", latent, w_uv, preferred_element_type=jnp.float32).astype(
-        jnp.bfloat16
-    )
-    head_out = head_out.reshape(head_out.shape[0], -1)
+    head_out = attend_call(lengths, queries, cache.swapaxes(1, 2), w_uv)
     return layer_call(
         head_out,
         residual_in.T,

time: 162 us -> 152 us (0.938)
  matrix products: 14.9 us -> 0 us
  Pallas kernels: 143 us -> 149 us
    dot_general x3 -> x0, matrix products: 14.9 us -> none  [the longest x1 6.73 us: shards(): jnp.einsum('rhl,rlk->rhk', attn_probs, cache[:, :, :latent_width], prefer...]
    pallas_call x0 -> x1, Pallas kernels: none -> 11.7 us  [attend_call(): pl.pallas_call(attend_kernel, out_shape=jax.ShapeDtypeStruct((HALF, 16 *...]
    pallas_call x1, Pallas kernels: 143 us -> 137 us  [layer_call(): pl.pallas_call(layer_kernel, out_shape=jax.ShapeDtypeStruct((OWN, 2 * HAL...]
where the time goes in v4:
time: 152 us
  Pallas kernels  149 us (98%)
  local copies, waits for them, and re-layouts  2.81 us (2%)
    pallas_call x1, Pallas kernels, layer_call(): pl.pallas_call(layer_kernel, out_shape=jax.ShapeDtypeStruct((OWN, 2 * HAL...  137 us
    pallas_call x1, Pallas kernels, attend_call(): pl.pallas_call(attend_kernel, out_shape=jax.ShapeDtypeStruct((HALF, 16 *...  11.7 us

profile of v4, /device:TPU:1, one launch (start us, length us, event | category | flops | bytes accessed | tf_op | source)
XLA Modules:
  0.0 151.8 jit_solution(5134156079303581886)
XLA Ops:
  0.0 1.3 reshape.9.gain_ref
  1.3 11.7 %shard_map.118.head_ref = bf16[64,2048]{1,0:T(8,128)(2,1)} custom-call(s32[64]{0:T(128)} %lengths_ref.1, bf16[64,16,576]{2,1,0:T(8,128)(2,1)} %queries_ref.1, bf16[64,576,128]{2,1,0:T(8,128)(2,1)} %bitcast.9, bf16[16,512,128]{2,1,0:T(8,128)(2,1)} %up_ref.1), custom_call_target="tpu_custom_call" | custom-call | flops 445644800 | bytes 14680064 | tf_op jit(solution)/shard_map/pallas_call | solution.py:697
  13.0 137.3 %shard_map.119 = bf16[448,128]{1,0:T(8,128)(2,1)} custom-call(bf16[64,2048]{1,0:T(8,128)(2,1)} %shard_map.118.head_ref, bf16[448,128]{1,0:T(8,128)(2,1)} %bitcast.15, bf16[1,448]{1,0:T(2,128)(2,1)} %reshape.9.gain_ref, s32[8,128]{1,0:T(8,128)} %bitcast.16, f32[8,128]{1,0:T(8,128)} %bitcast.17, bf16[448,2048]{1,0:T(8,128)(2,1)} %bitcast.14, ...), custom_call_target="tpu_custom_call" | custom-call | flops 14680064000 | bytes 16777216 | tf_op jit(solution)/shard_map/pallas_call | solution.py:760
  150.3 1.6 %copy.14 = bf16[128,448]{0,1:T(8,128)(2,1)} copy(bf16[128,448]{0,1:T(8,128)(2,1)} %bitcast.10) | data formatting | bytes 229376

commit v5 on v4

--- a/solution.py
+++ b/solution.py
@@ -554,11 +554,6 @@
             down_pairs[r, :, core * OWN : (core + 1) * OWN] = down[
                 :, (core * 8 + r) * OWN : (core * 8 + r + 1) * OWN
             ]
-    gather(0, 2, "relay")
-    gather(1, 2, "start")
-    shares(1, (0,), "start")
-    gather(0, 2, "near")
-    shares(0, (1, 3), "start")
     smalls(0, gates.at[col], "wait_recv")
     inverse_share.wait_recv()
     columns[...] = jnp.zeros_like(columns)
@@ -569,22 +564,27 @@
     columns[...] = columns[...].T
     for load in loads:
         load.wait()
+    gather(0, 2, "relay")
+    gather(0, 2, "near")
+    shares(0, (1, 3), "start")
     gather(0, 2, "far")
+    gather(1, 2, "start")
     shares(0, (2,), "start")
-    gather(1, 2, "relay")
+    shares(1, (0,), "start")
     experts_own(0)
     shares(0, (0, 1, 2, 3), "wait_recv")
     experts_theirs(0)
     down_theirs(0)
-    gather(1, 2, "near")
-    shares(1, (1, 3), "start")
+    gather(1, 2, "relay")
     for phase in range(3):
         gather(0, phase, "drain")
     shares(0, (0, 1, 2, 3), "wait_send")
+    gather(1, 2, "near")
+    shares(1, (1, 3), "start")
     down_own(0)
-    scatter(0, 0, "start")
     gather(1, 2, "far")
     shares(1, (2,), "start")
+    scatter(0, 0, "start")
     experts_own(1)
     shares(1, (0, 1, 2, 3), "wait_recv")
     experts_theirs(1)
@@ -662,50 +662,69 @@
 DMA = pltpu.SemaphoreType.DMA
 
 
-def attend_kernel(lengths_ref, queries_ref, cache_ref, up_ref, out_ref, latent):
-    step = pl.program_id(0)
+def attend_kernel(
+    lengths_ref, queries_hbm, cache_hbm, up_hbm, out_ref, queries, cache, up, latent, query_sems, cache_sems, up_sem
+):
+    def loads(group):
+        rows = pl.ds(group * GROUP, GROUP)
+        return (
+            pltpu.make_async_copy(queries_hbm.at[rows], queries.at[rows], query_sems.at[group]),
+            pltpu.make_async_copy(cache_hbm.at[rows], cache.at[rows], cache_sems.at[group]),
+        )
+
+    for group in range(HALF // GROUP):
+        for load in loads(group):
+            load.start()
+    load_up = pltpu.make_async_copy(up_hbm, up, up_sem)
+    load_up.start()
     lane = lax.broadcasted_iota(jnp.int32, (16, 128), 1)
-    scores = []
-    for i in range(GROUP):
-        score = jnp.dot(queries_ref[i], cache_ref[i], preferred_element_type=F32) * (HD + ROPE) ** (-0.5)
-        scores.append(jnp.where(lane < lengths_ref[step * GROUP + i], score, -jnp.inf))
-    scores = jnp.concatenate(scores, axis=0)
-    terms = jnp.exp(scores - jnp.max(scores, axis=1, keepdims=True))
-    probs = (terms / jnp.sum(terms, axis=1, keepdims=True)).astype(BF16)
-    for i in range(GROUP):
-        value = lax.dot_general(
-            probs[i * 16 : (i + 1) * 16],
-            cache_ref[i, 0:512],
-            (((1,), (1,)), ((), ())),
-            preferred_element_type=F32,
-        )
-        for k in range(4):
-            latent[k, pl.ds(pl.multiple_of((step * GROUP + i) * 16, 16), 16)] = value[:, k * 128 : k * 128 + 128]
-
-    @pl.when(step == HALF // GROUP - 1)
-    def _():
-        for head in range(16):
-            rows = jnp.concatenate(
-                [latent[k, pl.ds(head, HALF, stride=16)] for k in range(4)], axis=1
-            ).astype(BF16)
-            out_ref[:, head * HD : (head + 1) * HD] = jnp.dot(
-                rows, up_ref[head], preferred_element_type=F32
-            ).astype(BF16)
+
+    @pl.loop(0, HALF // GROUP)
+    def _(group):
+        for load in loads(group):
+            load.wait()
+        scores = []
+        for i in range(GROUP):
+            r = group * GROUP + i
+            score = jnp.dot(queries[r], cache[r], preferred_element_type=F32) * (HD + ROPE) ** (-0.5)
+            scores.append(jnp.where(lane < lengths_ref[r], score, -jnp.inf))
+        scores = jnp.concatenate(scores, axis=0)
+        terms = jnp.exp(scores - jnp.max(scores, axis=1, keepdims=True))
+        probs = (terms / jnp.sum(terms, axis=1, keepdims=True)).astype(BF16)
+        for i in range(GROUP):
+            r = group * GROUP + i
+            value = lax.dot_general(
+                probs[i * 16 : (i + 1) * 16],
+                cache[r, 0:512],
+                (((1,), (1,)), ((), ())),
+                preferred_element_type=F32,
+            )
+            for k in range(4):
+                latent[k, pl.ds(pl.multiple_of(r * 16, 16), 16)] = value[:, k * 128 : k * 128 + 128]
+
+    load_up.wait()
+    for head in range(16):
+        rows = jnp.concatenate([latent[k, pl.ds(head, HALF, stride=16)] for k in range(4)], axis=1).astype(BF16)
+        out_ref[:, head * HD : (head + 1) * HD] = jnp.dot(
+            rows, up[head], preferred_element_type=F32
+        ).astype(BF16)
 
 
 def attend_call(lengths, queries, cache, w_uv):
     return pl.pallas_call(
         attend_kernel,
         out_shape=jax.ShapeDtypeStruct((HALF, 16 * HD), BF16),
-        grid=(HALF // GROUP,),
-        in_specs=[
-            pl.BlockSpec(memory_space=pltpu.SMEM),
-            pl.BlockSpec((GROUP, 16, 576), lambda i: (i, 0, 0)),
-            pl.BlockSpec((GROUP, 576, 128), lambda i: (i, 0, 0)),
-            pl.BlockSpec((16, 512, HD), lambda i: (0, 0, 0)),
+        in_specs=[pl.BlockSpec(memory_space=pltpu.SMEM), ANY, ANY, ANY],
+        out_specs=VMEM,
+        scratch_shapes=[
+            pltpu.VMEM((HALF, 16, 576), BF16),
+            pltpu.VMEM((HALF, 576, 128), BF16),
+            pltpu.VMEM((16, 512, HD), BF16),
+            pltpu.VMEM((4, HALF * 16, 128), F32),
+            pltpu.SemaphoreType.DMA((HALF // GROUP,)),
+            pltpu.SemaphoreType.DMA((HALF // GROUP,)),
+            pltpu.SemaphoreType.DMA,
         ],
-        out_specs=pl.BlockSpec((HALF, 16 * HD), lambda i: (0, 0)),
-        scratch_shapes=[pltpu.VMEM((4, HALF * 16, 128), F32)],
         compiler_params=pltpu.CompilerParams(vmem_limit_bytes=58 * 2**20),
         cost_estimate=pl.CostEstimate(
             flops=2 * 64 * 16 * 128 * 1700, bytes_accessed=14 * 2**20, transcendentals=2**17

time: 152 us -> 148 us (0.974)
  Pallas kernels: 149 us -> 145 us
    pallas_call x1, Pallas kernels: 137 us -> 135 us  [layer_call(): pl.pallas_call(layer_kernel, out_shape=jax.ShapeDtypeStruct((OWN, 2 * HAL...]
    pallas_call x1, Pallas kernels: 11.7 us -> 9.73 us  [attend_call(): pl.pallas_call(attend_kernel, out_shape=jax.ShapeDtypeStruct((HALF, 16 *...]
where the time goes in v5:
time: 148 us
  Pallas kernels  145 us (98%)
  local copies, waits for them, and re-layouts  2.81 us (2%)
    pallas_call x1, Pallas kernels, layer_call(): pl.pallas_call(layer_kernel, out_shape=jax.ShapeDtypeStruct((OWN, 2 * HAL...  135 us
    pallas_call x1, Pallas kernels, attend_call(): pl.pallas_call(attend_kernel, out_shape=jax.ShapeDtypeStruct((HALF, 16 *...  9.73 us

profile of v5, /device:TPU:1, one launch (start us, length us, event | category | flops | bytes accessed | tf_op | source)
XLA Modules:
  0.0 147.6 jit_solution(7409004023810391798)
XLA Ops:
  0.0 1.3 reshape.9.gain_ref
  1.3 9.7 %shard_map.118.head_ref = bf16[64,2048]{1,0:T(8,128)(2,1)} custom-call(s32[64]{0:T(128)} %lengths_ref.1, bf16[64,16,576]{2,1,0:T(8,128)(2,1)} %queries_hbm.1, bf16[64,576,128]{2,1,0:T(8,128)(2,1)} %bitcast.9, bf16[16,512,128]{2,1,0:T(8,128)(2,1)} %up_hbm.1), custom_call_target="tpu_custom_call" | custom-call | flops 445644800 | bytes 14680064 | tf_op jit(solution)/shard_map/pallas_call | solution.py:714
  11.0 135.0 %shard_map.119 = bf16[448,128]{1,0:T(8,128)(2,1)} custom-call(bf16[64,2048]{1,0:T(8,128)(2,1)} %shard_map.118.head_ref, bf16[448,128]{1,0:T(8,128)(2,1)} %bitcast.15, bf16[1,448]{1,0:T(2,128)(2,1)} %reshape.9.gain_ref, s32[8,128]{1,0:T(8,128)} %bitcast.16, f32[8,128]{1,0:T(8,128)} %bitcast.17, bf16[448,2048]{1,0:T(8,128)(2,1)} %bitcast.14, ...), custom_call_target="tpu_custom_call" | custom-call | flops 14680064000 | bytes 16777216 | tf_op jit(solution)/shard_map/pallas_call | solution.py:779
  146.0 1.6 %copy.14 = bf16[128,448]{0,1:T(8,128)(2,1)} copy(bf16[128,448]{0,1:T(8,128)(2,1)} %bitcast.10) | data formatting | bytes 229376

commit v6 on v5

--- a/solution.py
+++ b/solution.py
@@ -24,8 +24,8 @@
 SUM_LANES = ((0, 512), (512, 384))
 LOW, HIGH, ALL = (0, 32), (32, 32), (0, 64)
 DIRECT_GATHERS = ((0, 0), (1, 0), (0, 1))
-DIRECT_SCATTERS = ((0, 2), (1, 1), (1, 2))
-GROUP = 8
+DIRECT_SCATTERS = ((0, 1), (0, 2), (1, 1), (1, 2))
+GROUP = 16
 
 
 class Place:
@@ -219,7 +219,7 @@
     heads, proj, part_sums, z_early, z_late, x_early, x_late, pair, pair_sib, pair_all, hidden, square,
     rows_buf, weights, down, down_pairs, total, acts, squares, inverses, gates, columns,
     from_sibling, mixed, mixed_sib,
-    load_sems, head_sems, flip_sems, sum_sems, pair_sems, proj_sems, small_send, small_recv,
+    load_sems, head_sems, flip_sems, sum_sems, pair_sems, proj_sems, head_share_sems, small_send, small_recv,
     send_sems, recv_sems, share_send, share_recv, back_send, back_recv, last_sems, *arrivals,
 ):
     here = Place()
@@ -290,7 +290,7 @@
     residual = square[...].T.astype(BF16)
     for half in range(2):
         pair[half, 0:HALF] = residual[half * HALF : (half + 1) * HALF, 0:OWN]
-        pair[half, HALF:80] = jnp.broadcast_to(gain_ref[...].astype(F32), (16, OWN)).astype(BF16)
+        pair[half, HALF:80] = jnp.broadcast_to(gain_ref[...].astype(F32)[None, :], (16, OWN)).astype(BF16)
     pair_copy = remote(pair.at[1 - side], pair_sib, pair_sems.at[0], pair_sems.at[1], sibling)
     pair_copy.start()
     proj_copy = remote(out_hbm, proj.at[side], proj_sems.at[0], proj_sems.at[1], sibling)
@@ -312,6 +312,11 @@
     rings[1].relay()
     rings[0].far()
     flips[3].start()
+    head_shares = []
+    for index, (which, z) in enumerate(((1, z_hi), (0, z_hi), (0, 1 - z_hi), (1, 1 - z_hi))):
+        ref = head_view(which, (z, slice(None), 1 - side), ALL)
+        head_shares.append(remote(ref, ref, head_share_sems.at[0, index], head_share_sems.at[1, index], sibling))
+    head_shares[0].start()
 
     pair_copy.wait_recv()
 
@@ -326,14 +331,13 @@
         pair_all[:, OWN:PAIR] = pair[1]
 
     rings[2].relay()
-    for ring in rings[1:]:
+    for ring, share_now in ((rings[1], head_shares[1]), (rings[2], head_shares[2])):
         ring.near()
         ring.far()
+        share_now.start()
     for flip in flips[1:]:
         flip.wait_recv()
-    theirs = heads.at[side, :, :, 1 - side]
-    head_share = remote(theirs, theirs, pair_sems.at[2], pair_sems.at[3], sibling)
-    head_share.start()
+    head_shares[3].start()
 
     load_proj.wait()
     proj_copy.wait_recv()
@@ -345,33 +349,38 @@
         )
         part_sums[source] = value.astype(BF16).reshape(4, HALF, PAIR)
 
-    project(side)
-    head_share.wait_recv()
-    project(1 - side)
-
-    def x_ring(kind, which, lead, arrived):
+
+    def x_ring(kind, index, which, lead, arrived):
         return kind(
             here,
             "x",
             lambda k, rows: part_sums.at[lead, here.coord["x"][k], pl.ds(*rows), pl.ds(*SUM_LANES[which])],
             (LOW, HIGH),
             arrived,
-            (sum_sems.at[0, which], sum_sems.at[1, which]),
+            (sum_sems.at[0, index], sum_sems.at[1, index]),
         )
 
     early_flip = remote(
         part_sums.at[1 - z_lo, :, :, pl.ds(*SUM_LANES[1])], z_early, flip_sems.at[0, 5], flip_sems.at[1, 5], flip_z
     )
+    first_ring = x_ring(RingScatter, 0, 0, side, x_early.at[0])
+    second_ring = x_ring(RingScatter, 2, 0, 1 - side, x_early.at[1])
+    project(side)
+    first_ring.start()
+    for copy in head_shares:
+        copy.wait_recv()
+    project(1 - side)
     early_flip.start()
-    early_ring = x_ring(RingScatter, 0, slice(None), x_early)
-    early_ring.start()
-    early_ring.relay()
+    second_ring.start()
+    first_ring.relay()
+    second_ring.relay()
     early_flip.wait_recv()
     mine = part_sums.at[z_lo, :, :, pl.ds(*SUM_LANES[1])]
     mine[...] = (mine[...].astype(F32) + z_early[...].astype(F32)).astype(BF16)
-    late_ring = x_ring(DirectScatter, 1, z_lo, x_late)
+    late_ring = x_ring(DirectScatter, 1, 1, z_lo, x_late)
     late_ring.start()
-    early_ring.finish()
+    first_ring.finish()
+    second_ring.finish()
     late_flip = remote(
         part_sums.at[1 - z_lo, x, :, pl.ds(*SUM_LANES[0])], z_late, flip_sems.at[0, 6], flip_sems.at[1, 6], flip_z
     )
@@ -598,7 +607,6 @@
     scatter(0, 0, "finish")
     scatter(0, 1, "start")
     scatter(1, 0, "relay")
-    scatter(0, 1, "relay")
     scatter(0, 1, "finish")
     scatter(0, 2, "start")
     final(0)
@@ -627,10 +635,10 @@
 
     for t in range(2):
         last(t).wait_send()
-    for ring in (*rings, early_ring, late_ring):
+    for ring in (*rings, first_ring, second_ring, late_ring):
         ring.drain()
     for copy in (
-        *flips, early_flip, late_flip, pair_copy, proj_copy, head_share, inverse_share,
+        *flips, *head_shares, early_flip, late_flip, pair_copy, proj_copy, inverse_share,
     ):
         copy.wait_send()
     smalls(0, gates.at[col], "wait_send")
@@ -739,7 +747,7 @@
         pltpu.VMEM((2, 4, HALF, PAIR), BF16),
         pltpu.VMEM((4, HALF, SUM_LANES[1][1]), BF16),
         pltpu.VMEM((HALF, SUM_LANES[0][1]), BF16),
-        pltpu.VMEM((2, 3, 2, 32, SUM_LANES[0][1]), BF16),
+        pltpu.VMEM((2, 2, 3, 32, SUM_LANES[0][1]), BF16),
         pltpu.VMEM((3, HALF, SUM_LANES[1][1]), BF16),
         pltpu.VMEM((2, 80, OWN), BF16),
         pltpu.VMEM((80, OWN), BF16),
@@ -762,9 +770,10 @@
         DMA((6,)),
         DMA((2, 3, 2, 3)),
         DMA((2, 7)),
-        DMA((2, 2, 2, 3)),
+        DMA((2, 3, 2, 3)),
         DMA((8,)),
         DMA((2,)),
+        DMA((2, 4)),
         DMA((3, 7)),
         DMA((3, 7)),
         DMA((2, 2, 3, 3, 2, 3)),
@@ -809,7 +818,7 @@
     return layer_call(
         head_out,
         residual_in.T,
-        norm_gain.reshape(1, OWN),
+        norm_gain,
         expert_ids.T,
         gate_vals.T,
         w_out.T,

time: 148 us -> 142 us (0.959)
  Pallas kernels: 145 us -> 141 us
    pallas_call x1, Pallas kernels: 135 us -> 132 us  [layer_call(): pl.pallas_call(layer_kernel, out_shape=jax.ShapeDtypeStruct((OWN, 2 * HAL...]
where the time goes in v6:
time: 142 us
  Pallas kernels  141 us (99%)
  local copies, waits for them, and re-layouts  1.55 us (1%)
    pallas_call x1, Pallas kernels, layer_call(): pl.pallas_call(layer_kernel, out_shape=jax.ShapeDtypeStruct((OWN, 2 * HAL...  132 us
    pallas_call x1, Pallas kernels, attend_call(): pl.pallas_call(attend_kernel, out_shape=jax.ShapeDtypeStruct((HALF, 16 *...  8.59 us

profile of v6, /device:TPU:1, one launch (start us, length us, event | category | flops | bytes accessed | tf_op | source)
XLA Modules:
  0.0 142.2 jit_solution(4103900654546504717)
XLA Ops:
  0.0 8.6 %shard_map.118.head_ref = bf16[64,2048]{1,0:T(8,128)(2,1)} custom-call(s32[64]{0:T(128)} %lengths_ref.1, bf16[64,16,576]{2,1,0:T(8,128)(2,1)} %queries_hbm.1, bf16[64,576,128]{2,1,0:T(8,128)(2,1)} %bitcast.9, bf16[16,512,128]{2,1,0:T(8,128)(2,1)} %up_hbm.1), custom_call_target="tpu_custom_call" | custom-call | flops 445644800 | bytes 14680064 | tf_op jit(solution)/shard_map/pallas_call | solution.py:722
  8.6 132.0 %shard_map.119 = bf16[448,128]{1,0:T(8,128)(2,1)} custom-call(bf16[64,2048]{1,0:T(8,128)(2,1)} %shard_map.118.head_ref, bf16[448,128]{1,0:T(8,128)(2,1)} %bitcast.15, bf16[448]{0:T(512)(128)(2,1)} %gain_ref.1, s32[8,128]{1,0:T(8,128)} %bitcast.16, f32[8,128]{1,0:T(8,128)} %bitcast.17, bf16[448,2048]{1,0:T(8,128)(2,1)} %bitcast.14, ...), custom_call_target="tpu_custom_call" | custom-call | flops 14680064000 | bytes 16777216 | tf_op jit(solution)/shard_map/pallas_call | solution.py:788
  140.6 1.6 %copy.14 = bf16[128,448]{0,1:T(8,128)(2,1)} copy(bf16[128,448]{0,1:T(8,128)(2,1)} %bitcast.10) | data formatting | bytes 229376
